TPU v7x, 256 devices: a whole 4x4x8 slice. The times are simulated.
256 devices in a mesh: frame: 16 (over z_lo, y), patch: 16 (over x, z_hi, core).
Axes of the slice: x: 4, y: 4, z: 8 (z_hi: 2, z_lo: 4; z = z_hi * 4 + z_lo), core: 2. Of those that a mesh axis runs over, the one named last changes fastest.
Arguments:
- latents: bfloat16 [2, 16, 1024, 1152], P(None, 'frame', 'patch'), may hold values from -6 to 6
- mod_spatial: float32 [2, 3, 1152], replicated, may hold values from -3 to 3
- mod_temporal: float32 [2, 3, 1152], replicated, may hold values from -3 to 3
- qkv_spatial: bfloat16 [1152, 1728], replicated, may hold values from -0.1875 to 0.1875
- out_spatial: bfloat16 [576, 1152], replicated, may hold values from -0.25 to 0.25
- qkv_temporal: bfloat16 [1152, 1728], replicated, may hold values from -0.1875 to 0.1875
- out_temporal: bfloat16 [576, 1152], replicated, may hold values from -0.25 to 0.25
- cotangent: bfloat16 [2, 16, 1024, 1152], P(None, 'frame', 'patch'), may hold values from -6 to 6
Outputs:
- grad_latents: bfloat16 [2, 16, 1024, 1152], P(None, 'frame', 'patch')
- grad_qkv_spatial: float32 [1152, 1728], P('frame', 'patch')
- grad_out_spatial: float32 [576, 1152], P('frame', 'patch')
- grad_qkv_temporal: float32 [1152, 1728], P('frame', 'patch')
- grad_out_temporal: float32 [576, 1152], P('frame', 'patch')
All inputs are finite; a program needn't handle non-finite values.
Results may differ from a plain program's by a relative error of at most 0.03.
Values may be sent and summed in bfloat16 or wider, within the bound.
A program may use at most 128 MiB of HBM per device.

v0:
```python
import jax
import jax.numpy as jnp
from jax import lax
from jax.sharding import PartitionSpec as P

HEAD_DIM = 72
HEADS = 8
ATT = 576


epsilon = 1e-06


def modulate(source, offset, stretch):
    centre = source - jnp.mean(source, axis=-1, keepdims=True)
    spread = jnp.mean(centre * centre, axis=-1, keepdims=True)
    return centre * lax.rsqrt(spread + epsilon) * (1.0 + stretch) + offset


def head_norm(projected):
    shaped = projected.reshape(projected.shape[:-1] + (3, HEADS, HEAD_DIM))
    paired = shaped[..., :2, :, :]
    paired = paired * lax.rsqrt(jnp.mean(paired * paired, axis=-1, keepdims=True) + epsilon)
    return jnp.concatenate([paired, shaped[..., 2:, :, :]], axis=-3).reshape(projected.shape)


def contract(left, right):
    return lax.dot_general(
        left, right, (((0, 1, 2), (0, 1, 2)), ((), ())), preferred_element_type=jnp.float32
    )


def attend_forward(packed):
    queries = packed[..., :HEAD_DIM]
    key_rows = packed[..., HEAD_DIM : 2 * HEAD_DIM]
    values = packed[..., 2 * HEAD_DIM :]
    scores = jnp.einsum(
        "nqd,nkd->nqk", queries, key_rows, preferred_element_type=jnp.float32
    ) * HEAD_DIM ** (-0.5)
    raised = jnp.exp(scores)
    softmax = raised / jnp.sum(raised, axis=-1, keepdims=True)
    return jnp.einsum(
        "nqk,nkd->nqd", softmax.astype(jnp.bfloat16), values, preferred_element_type=jnp.float32
    ).astype(jnp.bfloat16)


def attend_backward(packed, dout):
    queries = packed[..., :HEAD_DIM]
    key_rows = packed[..., HEAD_DIM : 2 * HEAD_DIM]
    values = packed[..., 2 * HEAD_DIM :]
    scale_factor = HEAD_DIM ** (-0.5)
    scores = (
        jnp.einsum("nqd,nkd->nqk", queries, key_rows, preferred_element_type=jnp.float32)
        * scale_factor
    )
    raised = jnp.exp(scores)
    softmax = raised / jnp.sum(raised, axis=-1, keepdims=True)
    rounded = softmax.astype(jnp.bfloat16)
    dvalues = jnp.einsum("nqk,nqd->nkd", rounded, dout, preferred_element_type=jnp.float32).astype(
        jnp.bfloat16
    )
    dweights = jnp.einsum("nqd,nkd->nqk", dout, values, preferred_element_type=jnp.float32)
    dscores = (
        softmax * (dweights - jnp.sum(dweights * softmax, axis=-1, keepdims=True)) * scale_factor
    ).astype(jnp.bfloat16)
    dqueries = jnp.einsum(
        "nqk,nkd->nqd", dscores, key_rows, preferred_element_type=jnp.float32
    ).astype(jnp.bfloat16)
    dkey_rows = jnp.einsum(
        "nqk,nqd->nkd", dscores, queries, preferred_element_type=jnp.float32
    ).astype(jnp.bfloat16)
    return jnp.concatenate([dqueries, dkey_rows, dvalues], axis=-1)


def branch_in(source, modulation, weight):
    offset = modulation[:, 0, None, None, :]
    stretch = modulation[:, 1, None, None, :]
    normed = modulate(source.astype(jnp.float32), offset, stretch).astype(jnp.bfloat16)
    projected = jnp.dot(normed, weight, preferred_element_type=jnp.float32)
    return (normed, projected, head_norm(projected).astype(jnp.bfloat16))


def branch_out(source, attended, modulation, weight):
    projected = jnp.dot(attended, weight, preferred_element_type=jnp.float32)
    return (source.astype(jnp.float32) + modulation[:, 2, None, None, :] * projected).astype(
        jnp.bfloat16
    )


def branch_back(source, normed, projected, dpacked, modulation, weight, upstream):
    pullback = jax.vjp(head_norm, projected)[1]
    dprojected = pullback(dpacked.astype(jnp.float32))[0].astype(jnp.bfloat16)
    grad_weight = contract(normed, dprojected)
    dnormed = lax.dot_general(
        dprojected, weight, (((3,), (1,)), ((), ())), preferred_element_type=jnp.float32
    )
    offset = modulation[:, 0, None, None, :]
    stretch = modulation[:, 1, None, None, :]

    def shaped(source_value):
        return modulate(source_value, offset, stretch)

    dsource = jax.vjp(shaped, source.astype(jnp.float32))[1](dnormed)[0]
    return (grad_weight, (upstream + dsource).astype(jnp.bfloat16))


def gate_back(upstream, attended, modulation, weight):
    scaled = (upstream * modulation[:, 2, None, None, :]).astype(jnp.bfloat16)
    grad_out = contract(attended, scaled)
    dattended = lax.dot_general(
        scaled, weight, (((3,), (1,)), ((), ())), preferred_element_type=jnp.float32
    ).astype(jnp.bfloat16)
    return (grad_out, dattended)


def body(
    latents,
    mod_spatial,
    mod_temporal,
    qkv_spatial,
    out_spatial,
    qkv_temporal,
    out_temporal,
    cotangent,
):
    clip_count, frames_here, patches_here = latents.shape[:3]
    normed_s, projected_s, packed_s = branch_in(latents, mod_spatial, qkv_spatial)
    item_rows = (
        packed_s.reshape(clip_count, frames_here, patches_here, 3, HEADS, HEAD_DIM)
        .transpose(0, 1, 4, 2, 3, 5)
        .reshape(clip_count * frames_here * HEADS, patches_here, 3 * HEAD_DIM)
    )
    spatial_items = lax.all_to_all(item_rows, "patch", split_axis=0, concat_axis=1, tiled=True)
    outputs_s = lax.all_to_all(
        attend_forward(spatial_items), "patch", split_axis=1, concat_axis=0, tiled=True
    )
    attended_s = (
        outputs_s.reshape(clip_count, frames_here, HEADS, patches_here, HEAD_DIM)
        .transpose(0, 1, 3, 2, 4)
        .reshape(clip_count, frames_here, patches_here, ATT)
    )
    middle = branch_out(latents, attended_s, mod_spatial, out_spatial)
    normed_t, projected_t, packed_t = branch_in(middle, mod_temporal, qkv_temporal)
    frame_rows = (
        packed_t.reshape(clip_count, frames_here, patches_here, 3, HEADS, HEAD_DIM)
        .transpose(0, 2, 4, 1, 3, 5)
        .reshape(clip_count, patches_here, HEADS, frames_here, 3 * HEAD_DIM)
    )
    temporal_items = lax.all_to_all(frame_rows, "frame", split_axis=1, concat_axis=3, tiled=True)
    layout = temporal_items.shape
    flat_rows = temporal_items.reshape(-1, layout[3], layout[4])
    outputs_t = attend_forward(flat_rows).reshape(layout[:4] + (HEAD_DIM,))
    returned_t = lax.all_to_all(outputs_t, "frame", split_axis=3, concat_axis=1, tiled=True)
    attended_t = returned_t.transpose(0, 3, 1, 2, 4).reshape(
        clip_count, frames_here, patches_here, ATT
    )
    upstream = cotangent.astype(jnp.float32)
    grad_out_t, dattended_t = gate_back(upstream, attended_t, mod_temporal, out_temporal)
    dframe = dattended_t.reshape(clip_count, frames_here, patches_here, HEADS, HEAD_DIM).transpose(
        0, 2, 3, 1, 4
    )
    dtemporal = lax.all_to_all(dframe, "frame", split_axis=1, concat_axis=3, tiled=True)
    dflat = attend_backward(flat_rows, dtemporal.reshape(-1, layout[3], HEAD_DIM)).reshape(layout)
    dreturned = lax.all_to_all(dflat, "frame", split_axis=3, concat_axis=1, tiled=True)
    dpacked_t = (
        dreturned.reshape(clip_count, patches_here, HEADS, frames_here, 3, HEAD_DIM)
        .transpose(0, 3, 1, 4, 2, 5)
        .reshape(clip_count, frames_here, patches_here, 3 * ATT)
    )
    grad_qkv_t, dmiddle = branch_back(
        middle, normed_t, projected_t, dpacked_t, mod_temporal, qkv_temporal, upstream
    )
    upstream_s = dmiddle.astype(jnp.float32)
    grad_out_s, dattended_s = gate_back(upstream_s, attended_s, mod_spatial, out_spatial)
    dpatch = (
        dattended_s.reshape(clip_count, frames_here, patches_here, HEADS, HEAD_DIM)
        .transpose(0, 1, 3, 2, 4)
        .reshape(clip_count * frames_here * HEADS, patches_here, HEAD_DIM)
    )
    dspatial = lax.all_to_all(dpatch, "patch", split_axis=0, concat_axis=1, tiled=True)
    dgrouped = lax.all_to_all(
        attend_backward(spatial_items, dspatial), "patch", split_axis=1, concat_axis=0, tiled=True
    )
    dpacked_s = (
        dgrouped.reshape(clip_count, frames_here, HEADS, patches_here, 3, HEAD_DIM)
        .transpose(0, 1, 3, 4, 2, 5)
        .reshape(clip_count, frames_here, patches_here, 3 * ATT)
    )
    grad_qkv_s, grad_latents = branch_back(
        latents, normed_s, projected_s, dpacked_s, mod_spatial, qkv_spatial, upstream_s
    )
    summed_rows = (
        lax.psum_scatter(
            grad_qkv_s.astype(jnp.bfloat16), "frame", scatter_dimension=0, tiled=True
        ).astype(jnp.float32),
        lax.psum_scatter(
            grad_out_s.astype(jnp.bfloat16), "frame", scatter_dimension=0, tiled=True
        ).astype(jnp.float32),
        lax.psum_scatter(
            grad_qkv_t.astype(jnp.bfloat16), "frame", scatter_dimension=0, tiled=True
        ).astype(jnp.float32),
        lax.psum_scatter(
            grad_out_t.astype(jnp.bfloat16), "frame", scatter_dimension=0, tiled=True
        ).astype(jnp.float32),
    )
    summed = (
        lax.psum_scatter(
            summed_rows[0].astype(jnp.bfloat16), "patch", scatter_dimension=1, tiled=True
        ).astype(jnp.float32),
        lax.psum_scatter(
            summed_rows[1].astype(jnp.bfloat16), "patch", scatter_dimension=1, tiled=True
        ).astype(jnp.float32),
        lax.psum_scatter(
            summed_rows[2].astype(jnp.bfloat16), "patch", scatter_dimension=1, tiled=True
        ).astype(jnp.float32),
        lax.psum_scatter(
            summed_rows[3].astype(jnp.bfloat16), "patch", scatter_dimension=1, tiled=True
        ).astype(jnp.float32),
    )
    return (grad_latents, summed[0], summed[1], summed[2], summed[3])


def solution(mesh):
    placed = (
        P(None, "frame", "patch", None),
        P(),
        P(),
        P(),
        P(),
        P(),
        P(),
        P(None, "frame", "patch", None),
    )
    return jax.shard_map(
        body,
        mesh=mesh,
        in_specs=placed,
        out_specs=(
            P(None, "frame", "patch", None),
            P("frame", "patch"),
            P("frame", "patch"),
            P("frame", "patch"),
            P("frame", "patch"),
        ),
        check_vma=False,
    )
```

profile of v0, /device:TPU:32, one launch (start us, length us, event | category | flops | bytes accessed | tf_op | source)
XLA Modules:
  0.0 562.6 jit_solution(16759014146334265004)
XLA Ops:
  10.3 4.5 convolution_bitcast_fusion.5
  18.5 30.5 %all_to_all.93 = bf16[16,64,216]{2,1,0:T(8,128)(2,1)S(1)} all-to-all(bf16[16,64,216]{2,1,0:T(8,128)(2,1)} %reshape.456), channel_id=1, replica_groups=mesh['frame'=16,'patch'=16] {'patch'}, dimensions={0} | all-to-all | bytes 884736 | tf_op jit(solution)/shard_map/all_to_all | solution.py:133
  49.8 2.0 copy-done.3
  53.7 2.3 reduce.16
  57.2 3.5 all-to-all-start.1
  60.7 1.9 fusion.36
  63.7 7.7 %all-to-all-done.1 = bf16[16,2,2304]{2,1,0:T(2,128)(2,1)S(1)} async-done(((bf16[16,2,2304]{2,1,0:T(2,128)(2,1)}), bf16[16,2,2304]{2,1,0:T(2,128)(2,1)S(1)}, u32[]{:S(2)}, u32[]{:S(2)}) %all-to-all-start.1) | async-done | bytes 147488 | tf_op jit(solution)/shard_map/all_to_all | solution.py:134
  71.4 6.7 %all-to-all-start.3 = ((bf16[2,64,8,1,72]{4,2,0,3,1:T(8,128)(2,1)}), bf16[2,64,8,1,72]{4,2,0,3,1:T(8,128)(2,1)S(1)}, u32[]{:S(2)}, u32[]{:S(2)}) async-start(bf16[2,64,8,1,72]{4,2,0,3,1:T(8,128)(2,1)} %copy.74), calls=%async_computation.3 | async-start | bytes 524288 | tf_op jit(solution)/shard_map/all_to_all | solution.py:162
  81.4 4.3 convolution_bitcast_fusion.4
  87.5 1.7 copy.94
  89.2 3.1 reshape.489
  92.4 7.5 %all-to-all-start.2 = ((bf16[2,64,8,1,216]{4,2,0,3,1:T(8,128)(2,1)}), bf16[2,64,8,1,216]{4,2,0,3,1:T(8,128)(2,1)}, u32[]{:S(2)}, u32[]{:S(2)}) async-start(bf16[2,64,8,1,216]{4,2,0,3,1:T(8,128)(2,1)} %reshape.489), calls=%async_computation.2 | async-start | bytes 1048576 | tf_op jit(solution)/shard_map/all_to_all | solution.py:149
  100.8 13.3 %all-to-all-done.2 = bf16[2,64,8,1,216]{4,2,0,3,1:T(8,128)(2,1)} async-done(((bf16[2,64,8,1,216]{4,2,0,3,1:T(8,128)(2,1)}), bf16[2,64,8,1,216]{4,2,0,3,1:T(8,128)(2,1)}, u32[]{:S(2)}, u32[]{:S(2)}) %all-to-all-start.2) | async-done | bytes 442400 | tf_op jit(solution)/shard_map/all_to_all | solution.py:149
  116.3 2.3 fusion.72
  118.7 2.1 fusion.82
  120.8 3.0 convolution_convert_fusion.3
  123.8 2.8 convolution_convert_fusion.2
  126.5 2.3 fusion.31
  128.8 2.3 convolution_convert_fusion.1
  132.8 18.9 %all_to_all.94 = bf16[2,4,8,16,216]{4,2,1,0,3:T(8,128)(2,1)S(1)} all-to-all(bf16[2,4,8,16,216]{4,2,1,0,3:T(8,128)(2,1)S(1)} %copy.77), channel_id=1, replica_groups=mesh['frame'=16,'patch'=16] {'frame'}, dimensions={3} | all-to-all | bytes 884736 | tf_op jit(solution)/shard_map/all_to_all | solution.py:164
  152.9 3.6 reshape.474
  156.4 2.6 copy.105
  161.8 1.9 convert_element_type.222
  163.7 4.1 fusion.4
  167.9 3.0 fusion.62
  173.1 19.5 %all_to_all.95 = bf16[16,64,72]{2,1,0:T(8,128)(2,1)S(1)} all-to-all(bf16[16,64,72]{2,1,0:T(8,128)(2,1)S(1)} %bitcast.295), channel_id=1, replica_groups=mesh['frame'=16,'patch'=16] {'patch'}, dimensions={0} | all-to-all | bytes 294912 | tf_op jit(solution)/shard_map/all_to_all | solution.py:180
  192.6 3.5 multiply_reduce_fusion
  200.5 4.1 reduce.17
  205.9 26.3 %all_to_all.96 = bf16[16,2,6912]{2,1,0:T(2,128)(2,1)S(1)} all-to-all(bf16[16,2,6912]{2,1,0:T(2,128)(2,1)S(1)} %reshape.506), channel_id=1, replica_groups=mesh['frame'=16,'patch'=16] {'patch'}, dimensions={0} | all-to-all | bytes 884736 | tf_op jit(solution)/shard_map/all_to_all | solution.py:181
  232.2 1.8 reshape.507
  234.7 1.7 reshape.475
  236.4 2.8 copy.84
  240.4 1.6 multiply_reduce_fusion.1
  244.1 3.4 fusion.3
  249.1 15.1 %all_to_all.97 = bf16[2,4,8,16,72]{4,2,1,0,3:T(8,128)(2,1)S(1)} all-to-all(bf16[2,4,8,16,72]{4,2,1,0,3:T(8,128)(2,1)S(1)} %copy.87), channel_id=1, replica_groups=mesh['frame'=16,'patch'=16] {'frame'}, dimensions={3} | all-to-all | bytes 294912 | tf_op jit(solution)/shard_map/all_to_all | solution.py:153
  265.1 1.6 fusion.11
  266.6 77.1 %fusion.110 = (bf16[48,1152]{1,0:T(8,128)(2,1)}, bf16[48,1152]{1,0:T(8,128)(2,1)S(1)}) fusion(bf16[576,1152]{1,0:T(8,128)(2,1)S(1)} %fusion.11, bf16[576,1152]{1,0:T(8,128)(2,1)S(1)} %fusion.12), kind=kCustom, calls=%all-reduce-scatter.2 | all-reduce-scatter fusion | flops 1769473 | bytes 2876416
  343.7 1.9 collective-permute-start.2
  346.6 1.9 collective-permute-start.1
  348.5 1.9 collective-permute-start.3
  350.4 1.9 collective-permute-start
  352.4 4.3 collective-permute-start.6
  356.7 3.7 collective-permute-start.5
  360.5 5.8 %collective-permute-start.4 = (bf16[48,1152]{1,0:T(8,128)(2,1)S(1)}, bf16[48,1152]{1,0:T(8,128)(2,1)S(1)}, u32[]{:S(2)}, u32[]{:S(2)}) collective-permute-start(bf16[48,1152]{1,0:T(8,128)(2,1)S(1)} %get-tuple-element.32), channel_id=1, source_target_pairs={{0,16},{16,32},{32,48},{48,64},{64,80},{80,96},{96,112},{112,128},... | collective-permute-start | bytes 331784
  366.4 1.9 collective-permute-start.7
  371.4 1.9 concatenate.30
  375.8 3.1 fusion.61
  380.3 172.3 %all-reduce.16.cloned.1.call-done = (bf16[72,1728]{1,0:T(8,128)(2,1)}, bf16[36,1152]{1,0:T(8,128)(2,1)}, bf16[72,1728]{1,0:T(8,128)(2,1)}, bf16[36,1152]{1,0:T(8,128)(2,1)}) async-done(((bf16[72,1728]{1,0:T(8,128)(2,1)}, bf16[36,1152]{1,0:T(8,128)(2,1)}, bf16[72,1728]{1,0:T(8,128)(2,1)}, bf16[36,1152]{1,0:T(8,128)(2,1)}), (bf16[72,1728]{1,0:T(8,128)(2,1)}, bf16[36,1152]{1,0:T(8,128)(2,1)}, ...) | async-done | bytes 663568
  (178 shorter events, 48.2 us)
Async XLA Ops:
  7.2 73.0 %copy-start = (bf16[576,1152]{1,0:T(8,128)(2,1)S(1)}, bf16[576,1152]{1,0:T(8,128)(2,1)}, u32[]{:S(2)}) copy-start(bf16[576,1152]{1,0:T(8,128)(2,1)} %param.12) | copy-start | bytes 3981316
  9.6 5.3 copy-start.32
  9.6 5.2 copy-start.28
  10.3 4.5 copy-start.18
  10.3 4.5 copy-start.22
  49.7 2.0 copy-start.3
  49.8 2.9 copy-start.30
  51.7 8.9 %copy-start.25 = (f32[2,3,1152]{2,0,1:T(2,128)S(1)}, f32[2,3,1152]{2,0,1:T(2,128)}, u32[]{:S(2)}) copy-start(f32[2,3,1152]{2,0,1:T(2,128)} %param.10) | copy-start | bytes 82948
  51.8 9.0 %copy-start.13 = (bf16[2,1,64,1152]{3,2,1,0:T(8,128)(2,1)S(1)}, bf16[2,1,64,1152]{3,2,1,0:T(8,128)(2,1)}, u32[]{:S(2)}) copy-start(bf16[2,1,64,1152]{3,2,1,0:T(8,128)(2,1)} %param.15) | copy-start | bytes 884740
  57.2 14.3 %all-to-all-start.1 = ((bf16[16,2,2304]{2,1,0:T(2,128)(2,1)}), bf16[16,2,2304]{2,1,0:T(2,128)(2,1)S(1)}, u32[]{:S(2)}, u32[]{:S(2)}) async-start(bf16[16,2,2304]{2,1,0:T(2,128)(2,1)} %reshape.504), calls=%async_computation.1 | async-start | bytes 294912 | tf_op jit(solution)/shard_map/all_to_all | solution.py:134
  60.7 10.7 %copy-start.20 = (f32[2,1152]{1,0:T(2,128)}, f32[2,1152]{1,0:T(2,128)S(1)}, u32[]{:S(2)}) copy-start(f32[2,1152]{1,0:T(2,128)S(1)} %get-tuple-element.34) | copy-start | bytes 27652
  60.7 20.2 %copy-start.24 = (f32[2,1152]{1,0:T(2,128)}, f32[2,1152]{1,0:T(2,128)S(1)}, u32[]{:S(2)}) copy-start(f32[2,1152]{1,0:T(2,128)S(1)} %get-tuple-element.35) | copy-start | bytes 27652
  60.7 19.4 %copy-start.2 = (bf16[2,1,64,1152]{3,2,1,0:T(8,128)(2,1)S(1)}, bf16[2,1,64,1152]{3,2,1,0:T(8,128)(2,1)}, u32[]{:S(2)}) copy-start(bf16[2,1,64,1152]{3,2,1,0:T(8,128)(2,1)} %param.8) | copy-start | bytes 884740
  71.4 20.9 %all-to-all-start.3 = ((bf16[2,64,8,1,72]{4,2,0,3,1:T(8,128)(2,1)}), bf16[2,64,8,1,72]{4,2,0,3,1:T(8,128)(2,1)S(1)}, u32[]{:S(2)}, u32[]{:S(2)}) async-start(bf16[2,64,8,1,72]{4,2,0,3,1:T(8,128)(2,1)} %copy.74), calls=%async_computation.3 | async-start | bytes 524288 | tf_op jit(solution)/shard_map/all_to_all | solution.py:162
  80.1 5.6 copy-start.15
  80.9 4.9 copy-start.26
  85.8 1.2 copy-start.7
  92.4 21.8 %all-to-all-start.2 = ((bf16[2,64,8,1,216]{4,2,0,3,1:T(8,128)(2,1)}), bf16[2,64,8,1,216]{4,2,0,3,1:T(8,128)(2,1)}, u32[]{:S(2)}, u32[]{:S(2)}) async-start(bf16[2,64,8,1,216]{4,2,0,3,1:T(8,128)(2,1)} %reshape.489), calls=%async_computation.2 | async-start | bytes 1048576 | tf_op jit(solution)/shard_map/all_to_all | solution.py:149
  99.9 279.4 %reduce-scatter.13.cloned.1.call-start = ((), (), s32[]{:S(2)}) async-start(), calls=%async_computation.11 | async-start | bytes 4386816 | tf_op jit(solution)/shard_map/reduce_scatter | solution.py:199
  100.8 17.9 %copy-start.16 = (bf16[2,16,4,8,1,72]{5,1,3,2,0,4:T(8,128)(2,1)S(1)}, bf16[2,16,4,8,1,72]{5,1,3,2,0,4:T(8,128)(2,1)}, u32[]{:S(2)}) copy-start(bf16[2,16,4,8,1,72]{5,1,3,2,0,4:T(8,128)(2,1)} %copy.75) | copy-start | bytes 442372
  156.4 2.6 copy-start.8
  167.8 211.4 %reduce-scatter.11.cloned.1.call-start = ((), (), s32[]{:S(2)}) async-start(), calls=%async_computation.10 | async-start | bytes 4386816 | tf_op jit(solution)/shard_map/reduce_scatter | solution.py:193
  167.9 3.0 copy-start.35
  167.9 3.0 copy-start.27
  171.2 21.4 %copy-start.31 = (f32[1024]{0:T(1024)S(1)}, f32[1024]{0:T(1024)}, u32[]{:S(2)}) copy-start(f32[1024]{0:T(1024)} %copy-done.30) | copy-start | bytes 12292
  192.6 3.5 copy-start.4
  236.4 4.0 copy-start.6
  239.2 2.8 copy-start.9
  242.7 1.3 copy-start.19
  242.8 1.3 copy-start.23
  242.8 1.3 copy-start.29
  247.4 1.2 copy-start.17
  247.5 17.0 %copy-start.14 = (bf16[2,1,64,1152]{3,2,1,0:T(8,128)(2,1)S(1)}, bf16[2,1,64,1152]{3,2,1,0:T(8,128)(2,1)}, u32[]{:S(2)}) copy-start(bf16[2,1,64,1152]{3,2,1,0:T(8,128)(2,1)} %param.15) | copy-start | bytes 884740
  247.5 17.0 %copy-start.21 = (f32[2,1152]{1,0:T(2,128)S(1)}, f32[2,1152]{1,0:T(2,128)}, u32[]{:S(2)}) copy-start(f32[2,1152]{1,0:T(2,128)} %copy-done.20) | copy-start | bytes 27652
  247.5 305.1 %all-reduce.16.cloned.1.call-start = ((), (), s32[]{:S(2)}) async-start(), calls=%async_computation.12 | async-start | bytes 1400832
  265.0 103.3 %copy-start.36 = (u32[256]{0:T(256)S(1)}, u32[256]{0:T(256)}, u32[]{:S(2)}) copy-start(u32[256]{0:T(256)} %constant.45) | copy-start | bytes 3076
  265.0 103.8 %copy-start.37 = (u32[256]{0:T(256)S(1)}, u32[256]{0:T(256)}, u32[]{:S(2)}) copy-start(u32[256]{0:T(256)} %constant.41) | copy-start | bytes 3076
  343.7 16.7 %collective-permute-start.2 = (bf16[48,1152]{1,0:T(8,128)(2,1)}, bf16[48,1152]{1,0:T(8,128)(2,1)S(1)}, u32[]{:S(2)}, u32[]{:S(2)}) collective-permute-start(bf16[48,1152]{1,0:T(8,128)(2,1)} %get-tuple-element.31), channel_id=1, source_target_pairs={{0,48},{16,64},{32,80},{48,96},{64,112},{80,128},{96,144},{112,160... | collective-permute-start | bytes 331784
  346.6 19.8 %collective-permute-start.1 = (bf16[48,1152]{1,0:T(8,128)(2,1)}, bf16[48,1152]{1,0:T(8,128)(2,1)S(1)}, u32[]{:S(2)}, u32[]{:S(2)}) collective-permute-start(bf16[48,1152]{1,0:T(8,128)(2,1)} %get-tuple-element.31), channel_id=1, source_target_pairs={{0,32},{16,48},{32,64},{48,80},{64,96},{80,112},{96,128},{112,144}... | collective-permute-start | bytes 331784
  348.5 8.2 %collective-permute-start.3 = (bf16[36,1152]{1,0:T(8,128)(2,1)S(1)}, bf16[36,1152]{1,0:T(8,128)(2,1)S(1)}, u32[]{:S(2)}, u32[]{:S(2)}) collective-permute-start(bf16[36,1152]{1,0:T(8,128)(2,1)S(1)} %slice.87), channel_id=1, source_target_pairs={{0,64},{16,80},{32,96},{48,112},{64,128},{80,144},{96,160},{112,17... | collective-permute-start | bytes 248840
  350.4 21.0 %collective-permute-start = (bf16[48,1152]{1,0:T(8,128)(2,1)}, bf16[48,1152]{1,0:T(8,128)(2,1)S(1)}, u32[]{:S(2)}, u32[]{:S(2)}) collective-permute-start(bf16[48,1152]{1,0:T(8,128)(2,1)} %get-tuple-element.31), channel_id=1, source_target_pairs={{0,16},{16,32},{32,48},{48,64},{64,80},{80,96},{96,112},{112,128},... | collective-permute-start | bytes 331784
  352.4 21.0 %collective-permute-start.6 = (bf16[48,1152]{1,0:T(8,128)(2,1)S(1)}, bf16[48,1152]{1,0:T(8,128)(2,1)S(1)}, u32[]{:S(2)}, u32[]{:S(2)}) collective-permute-start(bf16[48,1152]{1,0:T(8,128)(2,1)S(1)} %get-tuple-element.32), channel_id=1, source_target_pairs={{0,48},{16,64},{32,80},{48,96},{64,112},{80,128},{96,144},{112,160... | collective-permute-start | bytes 331784
  356.7 16.6 %collective-permute-start.5 = (bf16[48,1152]{1,0:T(8,128)(2,1)S(1)}, bf16[48,1152]{1,0:T(8,128)(2,1)S(1)}, u32[]{:S(2)}, u32[]{:S(2)}) collective-permute-start(bf16[48,1152]{1,0:T(8,128)(2,1)S(1)} %get-tuple-element.32), channel_id=1, source_target_pairs={{0,32},{16,48},{32,64},{48,80},{64,96},{80,112},{96,128},{112,144}... | collective-permute-start | bytes 331784
  360.5 12.9 %collective-permute-start.4 = (bf16[48,1152]{1,0:T(8,128)(2,1)S(1)}, bf16[48,1152]{1,0:T(8,128)(2,1)S(1)}, u32[]{:S(2)}, u32[]{:S(2)}) collective-permute-start(bf16[48,1152]{1,0:T(8,128)(2,1)S(1)} %get-tuple-element.32), channel_id=1, source_target_pairs={{0,16},{16,32},{32,48},{48,64},{64,80},{80,96},{96,112},{112,128},... | collective-permute-start | bytes 331784
  366.4 7.0 %collective-permute-start.7 = (bf16[36,1152]{1,0:T(8,128)(2,1)S(1)}, bf16[36,1152]{1,0:T(8,128)(2,1)S(1)}, u32[]{:S(2)}, u32[]{:S(2)}) collective-permute-start(bf16[36,1152]{1,0:T(8,128)(2,1)S(1)} %slice.88), channel_id=1, source_target_pairs={{0,64},{16,80},{32,96},{48,112},{64,128},{80,144},{96,160},{112,17... | collective-permute-start | bytes 248840
  375.8 3.1 copy-start.33
  375.8 3.5 copy-start.11
  375.8 179.7 %copy-start.1 = (bf16[576,1152]{1,0:T(8,128)(2,1)S(1)}, bf16[576,1152]{1,0:T(8,128)(2,1)}, u32[]{:S(2)}) copy-start(bf16[576,1152]{1,0:T(8,128)(2,1)} %param.12) | copy-start | bytes 3981316
  (4 other events, 3.5 us)
Sparse Core Ops, SparseCore 0:
  168.0 88.5 reduce-scatter.12
  259.1 103.0 reduce-scatter.10
  379.4 173.1 all-reduce.15
where the time goes:
time: 572 us; the launch traced here: 563 us
  waiting for transfers between devices  193 us (34%)
  blocking collectives  187 us (33%)
  local copies, waits for them, and re-layouts  50.3 us (9%)
  matrix products  50.1 us (9%)
  starting transfers between devices  41.3 us (7%)
  other arithmetic  22.9 us (4%)
  between operations  17.2 us (3%)
    unnamed x12, waiting for transfers between devices  172 us
    unnamed x1, blocking collectives  77.1 us
    all_to_all x1, blocking collectives, body(): lax.all_to_all(item_rows, 'patch', split_axis=0, concat_axis=1, tiled=True)  30.5 us
    all_to_all x1, blocking collectives, body(): lax.all_to_all(attend_backward(spatial_items, dspatial), 'patch', split_a...  26.3 us
    unnamed x9, starting transfers between devices  23.5 us
    all_to_all x1, blocking collectives, body(): lax.all_to_all(dpatch, 'patch', split_axis=0, concat_axis=1, tiled=True)  19.5 us
    all_to_all x1, blocking collectives, body(): lax.all_to_all(dflat, 'frame', split_axis=3, concat_axis=1, tiled=True)  18.9 us
    unnamed x89, local copies, waits for them, and re-layouts  18.4 us
  transfers between devices with their start and end apart: 14, of which 3 were waited for; matrix products, arithmetic and copies ran while one was open for 25% of the time, Pallas kernels for 0%

commit v1 on v0

v1 whole, which is shorter than its diff:
```python
import jax
import jax.numpy as jnp
from jax import lax
from jax.experimental import pallas as pl
from jax.experimental.pallas import tpu as pltpu
from jax.sharding import PartitionSpec as P

F32 = jnp.float32
BF = jnp.bfloat16
MESH = pl.DeviceIdType.MESH
HD = 72
HEADS = 8
ATT = 576
D = 1152
QKV = 1728
EPS = 1e-06
SCALE = HD**-0.5


def nn(a, b):
    return lax.dot_general(a, b, (((1,), (0,)), ((), ())), preferred_element_type=F32)


def nt(a, b):
    return lax.dot_general(a, b, (((1,), (1,)), ((), ())), preferred_element_type=F32)


def tn(a, b):
    return lax.dot_general(a, b, (((0,), (0,)), ((), ())), preferred_element_type=F32)


def owner(c, h):
    return (h // 2) * 4 + c * 2 + h % 2


def normalise(x):
    centre = x - jnp.mean(x, axis=-1, keepdims=True)
    r = lax.rsqrt(jnp.mean(centre * centre, axis=-1, keepdims=True) + EPS)
    return centre * r, r


def normalise_back(dn, stretch, xh, r):
    dx = dn * (1.0 + stretch)
    dx = dx - xh * jnp.mean(dx * xh, axis=-1, keepdims=True)
    dx = r * dx
    return dx - jnp.mean(dx, axis=-1, keepdims=True)


def inverse_norm(x):
    return lax.rsqrt(jnp.sum(x * x, axis=-1, keepdims=True) * (1.0 / HD) + EPS)


def head_back(dy, y, r):
    return r * (dy - y * (jnp.sum(dy * y, axis=-1, keepdims=True) * (1.0 / HD)))


def rounded(x):
    return x.astype(BF).astype(F32)


def zeros(*shape):
    return jnp.zeros(shape, F32)


def fold(x, near):
    n, _, w = x.shape
    far = x[:, :, near:]
    pad = 2 * near - w
    far = jnp.concatenate([far, zeros(n, 8, pad)], axis=-1)
    return jnp.concatenate([x[:, :, :near], far], axis=1)


def unfold(x, w):
    near = x.shape[-1]
    return jnp.concatenate([x[:, :8, :], x[:, 8:, : w - near]], axis=-1)


def widen(x, width):
    return jnp.concatenate([x, zeros(x.shape[0], width - x.shape[1])], axis=-1)


class Exchange:
    def __init__(self, send, recv, ssem, rsem, n, me, place):
        self.send, self.recv, self.ssem, self.rsem = send, recv, ssem, rsem
        self.n, self.me, self.place = n, me, place

    def copy(self, to, slot):
        return pltpu.make_async_remote_copy(
            src_ref=self.send.at[to],
            dst_ref=self.recv.at[slot],
            send_sem=self.ssem.at[to],
            recv_sem=self.rsem.at[slot],
            device_id=self.place(to),
            device_id_type=MESH,
        )

    def start(self):
        def step(i, carry):
            self.copy(lax.rem(self.me + i, self.n), self.me).start()
            return carry

        lax.fori_loop(1, self.n, step, 0)
        self.recv[self.me] = self.send[self.me]

    def wait(self):
        def step(i, carry):
            other = lax.rem(self.me + self.n - i, self.n)
            self.copy(other, other).wait()
            return carry

        lax.fori_loop(1, self.n, step, 0)


def kernel(
    lat, cot, mod_s, mod_t, wqs_h, wos_h, wqt_h, wot_h,
    gl, gqs, gos, gqt, got,
    wqs, wos, wqt, wot, wsem,
    normed, proj,
    a_s, a_r, b1_s, b1_r, b2_s, b2_r, t1_s, t1_r, t2_s, t2_r,
    c2_s, c2_r, c1_s, c1_r, dm_s, dm_r, d_s, d_r, xsems,
    q_b, k_b, v_b, rqk, att, do_b, kt_b, dq_f, dk_f, dv_f,
    ng, ngsem,
    xl, xrv, xr, xsem, lt,
    sx, rx, syq, ryq, syo, ryo, sxo, rxo, gys, gyr, sem4,
    szq, rzq, szo, rzo, gzs, gzr, sem8,
    fs, fr, fsem,
):
    f = lax.axis_index("frame")
    p = lax.axis_index("patch")
    core = lax.rem(p, 2)
    zh = lax.rem(lax.div(p, 2), 2)
    x = lax.div(p, 4)
    y = lax.rem(f, 4)
    zl = lax.div(f, 4)
    head = 2 * x + core
    clip_t = lax.div(f, 8)
    z = zh * 4 + zl

    loads = [
        pltpu.make_async_copy(src, dst, wsem.at[i])
        for i, (src, dst) in enumerate(
            ((wqs_h, wqs), (wos_h, wos), (wqt_h, wqt), (wot_h, wot))
        )
    ]
    for load in loads:
        load.start()

    barrier = pltpu.get_barrier_semaphore()

    def greet(i, carry):
        pl.semaphore_signal(
            barrier, inc=1, device_id={"frame": lax.rem(f + i, 16)}, device_id_type=MESH
        )
        pl.semaphore_signal(
            barrier, inc=1, device_id={"patch": lax.rem(p + i, 16)}, device_id_type=MESH
        )
        return carry

    lax.fori_loop(1, 16, greet, 0)

    def greet_z(i, carry):
        pl.semaphore_signal(
            barrier,
            inc=1,
            device_id={
                "frame": 4 * lax.rem(zl + i, 4) + y,
                "patch": 4 * x + 2 * (1 - zh) + core,
            },
            device_id_type=MESH,
        )
        return carry

    lax.fori_loop(1, 4, greet_z, 0)

    def on_patch(i):
        return {"patch": i}

    def on_frame(i):
        return {"frame": i}

    def on_x(i):
        return {"patch": 4 * i + 2 * zh + core}

    def on_y(i):
        return {"frame": 4 * zl + i}

    def on_z(i):
        return {
            "frame": 4 * lax.rem(i, 4) + y,
            "patch": 4 * x + 2 * lax.div(i, 4) + core,
        }

    ex_a = Exchange(a_s, a_r, xsems.at[0, 0], xsems.at[0, 1], 16, p, on_patch)
    ex_b1 = Exchange(b1_s, b1_r, xsems.at[1, 0], xsems.at[1, 1], 16, p, on_patch)
    ex_b2 = Exchange(b2_s, b2_r, xsems.at[2, 0], xsems.at[2, 1], 16, f, on_frame)
    ex_t1 = Exchange(t1_s, t1_r, xsems.at[3, 0], xsems.at[3, 1], 16, f, on_frame)
    ex_t2 = Exchange(t2_s, t2_r, xsems.at[4, 0], xsems.at[4, 1], 16, f, on_frame)
    ex_c2 = Exchange(c2_s, c2_r, xsems.at[5, 0], xsems.at[5, 1], 16, f, on_frame)
    ex_c1 = Exchange(c1_s, c1_r, xsems.at[6, 0], xsems.at[6, 1], 16, p, on_patch)
    ex_dm = Exchange(dm_s, dm_r, xsems.at[7, 0], xsems.at[7, 1], 16, f, on_frame)
    ex_d = Exchange(d_s, d_r, xsems.at[8, 0], xsems.at[8, 1], 16, p, on_patch)
    ex_xq = Exchange(sx, rx, sem4.at[0, 0], sem4.at[0, 1], 4, x, on_x)
    ex_yq = Exchange(syq, ryq, sem4.at[1, 0], sem4.at[1, 1], 4, y, on_y)
    ex_yo = Exchange(syo, ryo, sem4.at[2, 0], sem4.at[2, 1], 4, y, on_y)
    ex_xo = Exchange(sxo, rxo, sem4.at[3, 0], sem4.at[3, 1], 4, x, on_x)
    ex_gy = Exchange(gys, gyr, sem4.at[4, 0], sem4.at[4, 1], 4, y, on_y)
    ex_zq = Exchange(szq, rzq, sem8.at[0, 0], sem8.at[0, 1], 8, z, on_z)
    ex_zo = Exchange(szo, rzo, sem8.at[1, 0], sem8.at[1, 1], 8, z, on_z)
    ex_gz = Exchange(gzs, gzr, sem8.at[2, 0], sem8.at[2, 1], 8, z, on_z)

    for c in range(2):
        xh, _ = normalise(lat[c].astype(F32))
        normed[c] = (xh * (1.0 + mod_s[1, c : c + 1, :]) + mod_s[0, c : c + 1, :]).astype(BF)
    loads[0].wait()
    proj[...] = nt(normed[...].reshape(128, D), wqs[...])
    lane = lax.broadcasted_iota(jnp.int32, (128, 256), 1)
    for h in range(HEADS):
        q = proj[:, HD * h : HD * h + HD]
        k = proj[:, ATT + HD * h : ATT + HD * h + HD]
        v = proj[:, 2 * ATT + HD * h : 2 * ATT + HD * h + HD]
        rq = inverse_norm(q)
        rk = inverse_norm(k)
        row = jnp.concatenate([q * rq, k * rk, v, zeros(128, 40)], axis=-1)
        row = jnp.where(lane == 216, rq, row)
        row = jnp.where(lane == 217, rq - rounded(rq), row)
        row = jnp.where(lane == 218, rk, row)
        row = jnp.where(lane == 219, rk - rounded(rk), row)
        row = row.astype(BF)
        a_s[owner(0, h)] = row[:64]
        a_s[owner(1, h)] = row[64:]
    pl.semaphore_wait(barrier, 33)
    ex_a.start()

    for c in range(2):
        t1_s[8 * c : 8 * c + 8] = fold(lat[c].astype(F32).reshape(8, 8, D), 640).astype(BF)
        t2_s[8 * c : 8 * c + 8] = fold(cot[c].astype(F32).reshape(8, 8, D), 640).astype(BF)

    ex_a.wait()
    ex_t1.start()
    ex_t2.start()
    ng[p] = normed[zh]
    gather_z = pltpu.make_async_remote_copy(
        src_ref=normed.at[1 - zh],
        dst_ref=ng.at[p],
        send_sem=ngsem.at[0, 0],
        recv_sem=ngsem.at[1, 0],
        device_id={"patch": 4 * x + 2 * (1 - zh) + core},
        device_id_type=MESH,
    )
    gather_z.start()

    for part in range(4):
        rows = a_r[4 * part : 4 * part + 4].reshape(256, 256).astype(F32)
        at = pl.ds(256 * part, 256)
        q_b[at, :] = rows[:, 0:HD].astype(BF)
        k_b[at, :] = rows[:, HD : 2 * HD].astype(BF)
        v_b[at, :] = rows[:, 2 * HD : 3 * HD].astype(BF)
        rqk[at, 0:1] = rows[:, 216:217] + rows[:, 217:218]
        rqk[at, 1:2] = rows[:, 218:219] + rows[:, 219:220]

    def attend(i, carry):
        at = pl.ds(pl.multiple_of(i * 256, 256), 256)
        e = jnp.exp(nt(q_b[at, :], k_b[...]) * SCALE)
        weights = (e * (1.0 / jnp.sum(e, axis=-1, keepdims=True))).astype(BF)
        att[at, :] = nn(weights, v_b[...])
        return carry

    lax.fori_loop(0, 4, attend, 0)
    pieces = att[...].reshape(16, 4, 16, HD)
    row = [pieces[:, j].reshape(256, HD) for j in range(4)] + [zeros(256, 96)]
    b1_s[...] = jnp.concatenate(row, axis=-1).astype(BF).reshape(16, 16, 384)
    ex_b1.start()
    ex_b1.wait()
    for c in range(2):
        blocks = [b1_r[owner(c, h)].astype(F32) for h in range(HEADS)]
        rows = [
            jnp.concatenate([b[:, HD * j : HD * j + HD] for b in blocks], axis=-1)
            for j in range(4)
        ]
        tokens = jnp.concatenate(rows, axis=0).reshape(8, 8, ATT)
        b2_s[8 * c : 8 * c + 8] = fold(tokens, 384).astype(BF)
    ex_b2.start()

    gather_z.wait()

    def gather_copy(block, other, slot):
        return pltpu.make_async_remote_copy(
            src_ref=ng.at[block],
            dst_ref=ng.at[block],
            send_sem=ngsem.at[0, slot],
            recv_sem=ngsem.at[1, slot],
            device_id={"patch": other},
            device_id_type=MESH,
        )

    def gather_x(i, s, back):
        other = lax.rem(x + i, 4)
        block = lax.rem(x + 4 - i, 4) if back else x
        return gather_copy(4 * block + 2 * s + core, 4 * other + 2 * zh + core, 2 * i - 1 + s)

    for i in range(1, 4):
        for s in range(2):
            gather_x(i, s, False).start()

    def pick(ref, i):
        return jnp.where(clip_t == 0, ref[i, 0:1, :], ref[i, 1:2, :])

    gate_s = pick(mod_s, 2)
    shift_t, stretch_t, gate_t = pick(mod_t, 0), pick(mod_t, 1), pick(mod_t, 2)
    ex_t1.wait()
    ex_t2.wait()
    lat_t = unfold(t1_r[...].astype(F32), D).reshape(128, D)
    cot_t = unfold(t2_r[...].astype(F32), D).reshape(128, D)
    scaled_t = (cot_t * gate_t).astype(BF)
    for load in loads[1:]:
        load.wait()
    dout_t = nt(scaled_t, wot[...])
    ex_b2.wait()
    att_s = unfold(b2_r[...].astype(F32), ATT).reshape(128, ATT)
    middle = rounded(lat_t + gate_s * nn(att_s.astype(BF), wos[...]))
    xh_t, r_t = normalise(middle)
    normed_t = (xh_t * (1.0 + stretch_t) + shift_t).astype(BF)
    proj[...] = nt(normed_t, wqt[...])
    same = lax.rem(lax.broadcasted_iota(jnp.int32, (128, 128), 0), 8) == lax.rem(
        lax.broadcasted_iota(jnp.int32, (128, 128), 1), 8
    )
    att_parts, dq_parts, dk_parts, dv_parts = [], [], [], []
    for h in range(HEADS):
        q = proj[:, HD * h : HD * h + HD]
        k = proj[:, ATT + HD * h : ATT + HD * h + HD]
        v = proj[:, 2 * ATT + HD * h : 2 * ATT + HD * h + HD].astype(BF)
        rq = inverse_norm(q)
        rk = inverse_norm(k)
        q = q * rq
        k = k * rk
        qb, kb = q.astype(BF), k.astype(BF)
        e = jnp.where(same, jnp.exp(nt(qb, kb) * SCALE), 0.0)
        soft = e * (1.0 / jnp.sum(e, axis=-1, keepdims=True))
        soft_b = soft.astype(BF)
        att_parts.append(nn(soft_b, v))
        do = dout_t[:, HD * h : HD * h + HD].astype(BF)
        dp = nt(do, v)
        ds = (soft * (dp - jnp.sum(dp * soft, axis=-1, keepdims=True)) * SCALE).astype(BF)
        dq_parts.append(head_back(rounded(nn(ds, kb)), q, rq))
        dk_parts.append(head_back(rounded(tn(ds, qb)), k, rk))
        dv_parts.append(tn(soft_b, do))
    att_t = jnp.concatenate(att_parts, axis=-1)
    dproj_t = jnp.concatenate(dq_parts + dk_parts + dv_parts, axis=-1)
    dn = nn(dproj_t.astype(BF), wqt[...])
    dmiddle = rounded(cot_t + normalise_back(dn, stretch_t, xh_t, r_t))
    scaled_s = (dmiddle * gate_s).astype(BF)
    datt = nt(scaled_s, wos[...])
    c2_s[...] = fold(datt.reshape(16, 8, ATT), 384).astype(BF)
    ex_c2.start()

    for i in range(1, 4):
        for s in range(2):
            gather_x(i, s, True).wait()

    def spread_rows(a):
        parts = []
        for yy in range(4):
            for zz in range(4):
                at = 36 * (4 * zz + yy)
                parts += [a[:, at : at + 36], zeros(128, 4)]
        return parts

    xl[core] = jnp.concatenate(
        [normed_t.astype(F32)] + spread_rows(att_t) + spread_rows(att_s), axis=-1
    ).astype(BF)
    st, ss = scaled_t.astype(F32), scaled_s.astype(F32)
    for cc in range(2):
        parts = []
        for b in range(8):
            at = 108 * (2 * b + cc)
            parts += [dproj_t[:, at : at + 108], zeros(128, 20)]
        for full in (st, ss):
            parts += [full[:, HD * (2 * b + cc) : HD * (2 * b + cc) + HD] for b in range(8)]
            parts += [zeros(128, 64)]
        xrv[cc] = jnp.concatenate(parts, axis=-1).astype(BF)
    xr[core] = xrv[core]

    def pair_copies(slot):
        there = {"patch": p + 1 - 2 * core}
        return [
            pltpu.make_async_remote_copy(
                src_ref=src,
                dst_ref=dst.at[slot],
                send_sem=xsem.at[0, i],
                recv_sem=xsem.at[1, i],
                device_id=there,
                device_id_type=MESH,
            )
            for i, (src, dst) in enumerate(((xl.at[core], xl), (xrv.at[1 - core], xr)))
        ]

    for copy in pair_copies(core):
        copy.start()
    dm_s[...] = fold(dmiddle.reshape(16, 8, D), 640).astype(BF)
    ex_c2.wait()
    tokens = unfold(c2_r[...].astype(F32), ATT).reshape(2, 64, ATT)
    for c in range(2):
        for h in range(HEADS):
            part = tokens[c][:, HD * h : HD * h + HD].reshape(4, 16, HD)
            row = jnp.concatenate([part[j] for j in range(4)] + [zeros(16, 96)], axis=-1)
            c1_s[owner(c, h)] = row.astype(BF)
    ex_c1.start()
    ex_dm.start()

    def gather_core(i, back):
        side = 1 - core if back else core
        return gather_copy(2 * i + side, p + 1 - 2 * core, 7 + i)

    for i in range(8):
        gather_core(i, False).start()

    for copy in pair_copies(1 - core):
        copy.wait()
    lt[...] = jnp.transpose(xl[...].reshape(256, 2432).astype(F32)).astype(BF)
    right = xr[...].reshape(256, 2304)
    for i in range(4):
        g = nn(lt[0:D, :], right[:, 256 * i : 256 * i + 256]).astype(F32)
        g = g.reshape(4, 4, HD, 256)
        for yy in range(4):
            sx[i, 288 * yy : 288 * yy + 288, :] = g[:, yy].reshape(288, 256).astype(BF)
    ex_xq.start()
    for i in range(2):
        g = nn(lt[D + 640 * i : D + 640 * i + 640, :], right[:, 1024 + 640 * i : 1664 + 640 * i])
        for yy in range(4):
            syo[yy, 160 * i : 160 * i + 160, :] = g[160 * yy : 160 * yy + 160].astype(BF)
    ex_yo.start()

    for part in range(4):
        at = pl.ds(256 * part, 256)
        kt_b[:, at] = jnp.transpose(widen(k_b[at, :].astype(F32), 128)).astype(BF)
    ex_c1.wait()
    got_do = c1_r[...].astype(F32)
    parts = [got_do[:, :, HD * j : HD * j + HD] for j in range(4)]
    do_b[...] = jnp.stack(parts, axis=1).reshape(1024, HD).astype(BF)
    dk_f[...] = jnp.zeros_like(dk_f)
    dv_f[...] = jnp.zeros_like(dv_f)

    def attend_back(i, carry):
        at = pl.ds(pl.multiple_of(i * 256, 256), 256)
        qb, dob = q_b[at, :], do_b[at, :]
        e = jnp.exp(nt(k_b[...], qb) * SCALE)
        soft = e * (1.0 / jnp.sum(e, axis=0, keepdims=True))
        dv_f[...] += nn(soft.astype(BF), dob)
        dp = nt(v_b[...], dob)
        ds = (soft * (dp - jnp.sum(dp * soft, axis=0, keepdims=True)) * SCALE).astype(BF)
        dk_f[...] += nn(ds, qb)
        dq_f[at, :] = jnp.transpose(nn(kt_b[...], ds))[:, :HD]
        return carry

    lax.fori_loop(0, 4, attend_back, 0)
    for part in range(4):
        at = pl.ds(256 * part, 256)
        dq = head_back(rounded(dq_f[at, :]), q_b[at, :].astype(F32), rqk[at, 0:1])
        dk = head_back(rounded(dk_f[at, :]), k_b[at, :].astype(F32), rqk[at, 1:2])
        row = jnp.concatenate([dq, dk, dv_f[at, :], zeros(256, 40)], axis=-1).astype(BF)
        d_s[4 * part : 4 * part + 4] = row.reshape(4, 64, 256)
    ex_d.start()

    ex_xq.wait()
    for yy in range(4):
        at = pl.ds(288 * yy, 288)
        syq[yy] = sum(rx[i, at, :].astype(F32) for i in range(4)).astype(BF)
    ex_yq.start()
    ex_yo.wait()
    total = sum(ryo[i].astype(F32) for i in range(4))
    for i in range(4):
        sxo[i] = widen(total[:, 144 * i : 144 * i + 144], 256).astype(BF)
    ex_xo.start()

    for i in range(8):
        gather_core(i, True).wait()
    g = tn(ng[...].reshape(1024, D), d_s[...].reshape(1024, 256)).reshape(4, 4, HD, 256)
    for yy in range(4):
        gys[yy] = g[:, yy].reshape(288, 256).astype(BF)
    ex_gy.start()

    ex_yq.wait()
    total = sum(ryq[i].astype(F32) for i in range(4))
    for i in range(8):
        zz, s = i % 4, i // 4
        part = total[HD * zz : HD * zz + HD, 128 * s : 128 * s + 128]
        szq[i] = jnp.concatenate([part, zeros(8, 128)], axis=0).astype(BF)
    ex_zq.start()
    ex_xo.wait()
    total = sum(rxo[i].astype(F32) for i in range(4))
    for i in range(8):
        zz, s = i % 4, i // 4
        part = total[:, HD * s : HD * s + HD]
        part = jnp.concatenate(
            [part[40 * zz : 40 * zz + 40], part[160 + 40 * zz : 200 + 40 * zz]], axis=0
        )
        szo[i] = widen(part, 128).astype(BF)
    ex_zo.start()

    ex_d.wait()
    parts = []
    for c in range(2):
        blocks = [d_r[owner(c, h)].astype(F32) for h in range(HEADS)]
        parts.append(
            jnp.concatenate(
                [b[:, HD * j : HD * j + HD] for j in range(3) for b in blocks], axis=-1
            )
        )
    dn = nn(jnp.concatenate(parts, axis=0).astype(BF), wqs[...])
    ex_dm.wait()
    dmid = unfold(dm_r[...].astype(F32), D).reshape(2, 64, D)
    for c in range(2):
        xh, r = normalise(lat[c].astype(F32))
        back = normalise_back(dn[64 * c : 64 * c + 64], mod_s[1, c : c + 1, :], xh, r)
        gl[c] = (dmid[c] + back).astype(BF)

    ex_gy.wait()
    total = sum(gyr[i].astype(F32) for i in range(4))
    cols = [total[:, 36 * b : 36 * b + 36] for b in range(6)]
    sides = [
        jnp.concatenate([cols[s], cols[2 + s], cols[4 + s], zeros(288, 20)], axis=-1)
        for s in range(2)
    ]
    for i in range(8):
        zz, s = i % 4, i // 4
        part = sides[s][HD * zz : HD * zz + HD]
        gzs[i] = jnp.concatenate([part, zeros(8, 128)], axis=0).astype(BF)
    ex_gz.start()

    ex_zq.wait()
    total = sum(rzq[i].astype(F32) for i in range(8))
    gqt[...] = total[:HD, :108]
    ex_zo.wait()
    total = sum(rzo[i].astype(F32) for i in range(8))
    got[...] = total[:36, :HD]
    gos[...] = total[40:76, :HD]

    ex_gz.wait()
    total = sum(gzr[i].astype(F32) for i in range(8))
    for j in range(3):
        fs[j] = widen(total[:HD, 36 * j : 36 * j + 36], 128)

    def final_send(j):
        block = 16 * j + 2 * head + zh
        to, slot = lax.div(block, 3), lax.rem(block, 3)
        return to, slot, pltpu.make_async_remote_copy(
            src_ref=fs.at[j],
            dst_ref=fr.at[slot],
            send_sem=fsem.at[0, j],
            recv_sem=fsem.at[1, slot],
            device_id={"patch": to},
            device_id_type=MESH,
        )

    for j in range(3):
        to, slot, copy = final_send(j)

        @pl.when(to != p)
        def _():
            copy.start()

        @pl.when(to == p)
        def _():
            fr[slot] = fs[j]

    for j in range(3):
        to, slot, copy = final_send(j)

        @pl.when(to != p)
        def _():
            copy.wait_send()

    for slot in range(3):
        block = 3 * p + slot
        left = lax.rem(block, 16)
        src = lax.div(left, 4) * 4 + lax.rem(left, 2) * 2 + lax.rem(lax.div(left, 2), 2)

        @pl.when(src != p)
        def _():
            pltpu.make_async_remote_copy(
                src_ref=fs.at[0],
                dst_ref=fr.at[slot],
                send_sem=fsem.at[0, 0],
                recv_sem=fsem.at[1, slot],
                device_id={"patch": src},
                device_id_type=MESH,
            ).wait_recv()

    gqs[...] = jnp.concatenate([fr[j][:, :36] for j in range(3)], axis=-1)


def body(lat, mod_s, mod_t, wqs, wos, wqt, wot, cot):
    vmem = pl.BlockSpec(memory_space=pltpu.VMEM)
    hbm = pl.BlockSpec(memory_space=pl.ANY)
    dma = pltpu.SemaphoreType.DMA

    def buf(*shape):
        return pltpu.VMEM(shape, BF)

    def wide(*shape):
        return pltpu.VMEM(shape, F32)

    outs = pl.pallas_call(
        kernel,
        out_shape=(
            jax.ShapeDtypeStruct((2, 64, D), BF),
            jax.ShapeDtypeStruct((72, 108), F32),
            jax.ShapeDtypeStruct((36, 72), F32),
            jax.ShapeDtypeStruct((72, 108), F32),
            jax.ShapeDtypeStruct((36, 72), F32),
        ),
        in_specs=[vmem] * 4 + [hbm] * 4,
        out_specs=(vmem,) * 5,
        scratch_shapes=[
            buf(QKV, D), buf(ATT, D), buf(QKV, D), buf(ATT, D), dma((4,)),
            buf(2, 64, D), wide(128, QKV),
            buf(16, 64, 256), buf(16, 64, 256),
            buf(16, 16, 384), buf(16, 16, 384),
            buf(16, 16, 384), buf(16, 16, 384),
            buf(16, 16, 640), buf(16, 16, 640),
            buf(16, 16, 640), buf(16, 16, 640),
            buf(16, 16, 384), buf(16, 16, 384),
            buf(16, 16, 384), buf(16, 16, 384),
            buf(16, 16, 640), buf(16, 16, 640),
            buf(16, 64, 256), buf(16, 64, 256),
            dma((9, 2, 16)),
            buf(1024, HD), buf(1024, HD), buf(1024, HD), wide(1024, 2), wide(1024, HD),
            buf(1024, HD), buf(128, 1024), wide(1024, HD), wide(1024, HD), wide(1024, HD),
            buf(16, 64, D), dma((2, 15)),
            buf(2, 128, 2432), buf(2, 128, 2304), buf(2, 128, 2304), dma((2, 2)),
            buf(2432, 256),
            buf(4, 1152, 256), buf(4, 1152, 256),
            buf(4, 288, 256), buf(4, 288, 256),
            buf(4, 320, 640), buf(4, 320, 640),
            buf(4, 320, 256), buf(4, 320, 256),
            buf(4, 288, 256), buf(4, 288, 256),
            dma((5, 2, 4)),
            buf(8, 80, 128), buf(8, 80, 128),
            buf(8, 80, 128), buf(8, 80, 128),
            buf(8, 80, 128), buf(8, 80, 128),
            dma((3, 2, 8)),
            wide(3, 72, 128), wide(3, 72, 128), dma((2, 3)),
        ],
        compiler_params=pltpu.CompilerParams(
            collective_id=0, has_side_effects=True, vmem_limit_bytes=60 * 1024 * 1024
        ),
    )(
        lat.reshape(2, 64, D),
        cot.reshape(2, 64, D),
        mod_s.transpose(1, 0, 2),
        mod_t.transpose(1, 0, 2),
        wqs.T,
        wos,
        wqt.T,
        wot,
    )
    return (outs[0].reshape(2, 1, 64, D),) + tuple(outs[1:])


def solution(mesh):
    tokens = P(None, "frame", "patch", None)
    return jax.shard_map(
        body,
        mesh=mesh,
        in_specs=(tokens,) + (P(),) * 6 + (tokens,),
        out_specs=(tokens,) + (P("frame", "patch"),) * 4,
        check_vma=False,
    )
```

time: 572 us -> 147 us (0.26); the launches traced: 563 us -> 145 us
  waiting for transfers between devices: 193 us -> 0 us
  blocking collectives: 187 us -> 0 us
  Pallas kernels: 0 us -> 137 us
  matrix products: 50.1 us -> 0 us
  local copies, waits for them, and re-layouts: 50.3 us -> 7.14 us
  starting transfers between devices: 41.3 us -> 0 us
  other arithmetic: 22.9 us -> 0 us
  between operations: 17.2 us -> 0.64 us
    unnamed x12 -> x0, waiting for transfers between devices: 172 us -> none
    pallas_call x0 -> x1, Pallas kernels: none -> 137 us  [body(): pl.pallas_call(kernel, out_shape=(jax.ShapeDtypeStruct((2, 64, D), BF), j...]
    all_to_all x5 -> x0, blocking collectives: 110 us -> none  [the longest x1 30.5 us: body(): lax.all_to_all(item_rows, 'patch', split_axis=0, concat_axis=1, tiled=True)]
    unnamed x1 -> x0, blocking collectives: 77.1 us -> none
    dot_general x23 -> x0, matrix products: 47.8 us -> none  [the longest x4 9.63 us: contract(): lax.dot_general(left, right, (((0, 1, 2), (0, 1, 2)), ((), ())), preferre...]
    unnamed x9 -> x0, starting transfers between devices: 23.5 us -> none
    all_to_all x3 -> x0, waiting for transfers between devices: 21.1 us -> none  [the longest x1 13.3 us: body(): lax.all_to_all(frame_rows, 'frame', split_axis=1, concat_axis=3, tiled=True)]
    all_to_all x3 -> x0, starting transfers between devices: 17.7 us -> none  [the longest x1 7.54 us: body(): lax.all_to_all(frame_rows, 'frame', split_axis=1, concat_axis=3, tiled=True)]
  transfers between devices with their start and end apart: 14 -> 0, of which waited for: 3 -> 0; matrix products, arithmetic and copies ran while one was open for 25% -> 0% of each run, Pallas kernels for 0% -> 0%
where the time goes in v1:
time: 147 us; the launch traced here: 145 us
  Pallas kernels  137 us (93%)
  local copies, waits for them, and re-layouts  7.14 us (5%)
    pallas_call x1, Pallas kernels, body(): pl.pallas_call(kernel, out_shape=(jax.ShapeDtypeStruct((2, 64, D), BF), j...  137 us
    unnamed x5, local copies, waits for them, and re-layouts  7.14 us

profile of v1, /device:TPU:32, one launch (start us, length us, event | category | flops | bytes accessed | tf_op | source)
XLA Modules:
  0.0 145.2 jit_solution(7229241499948517717)
XLA Ops:
  0.6 137.4 %shard_map.119 = (bf16[2,64,1152]{2,1,0:T(8,128)(2,1)}, f32[72,108]{1,0:T(8,128)}, f32[36,72]{1,0:T(8,128)}, f32[72,108]{1,0:T(8,128)}, f32[36,72]{1,0:T(8,128)}) custom-call(bf16[2,64,1152]{2,1,0:T(8,128)(2,1)} %bitcast.11, bf16[2,64,1152]{2,1,0:T(8,128)(2,1)} %bitcast.12, f32[3,2,1152]{2,1,0:T(2,128)} %bitcast.14, f32[3,2,1152]{2,1,0:T(2,128)} %bitcast.15, ...), custom_call_target="tpu_custom_call" | custom-call | tf_op jit(solution)/shard_map/pallas_call | solution.py:603
  138.0 1.7 %copy.19 = bf16[2,1,64,1152]{3,2,1,0:T(8,128)(2,1)} copy(bf16[2,1,64,1152]{3,2,1,0:T(8,128)(2,1)} %bitcast.13) | data formatting | bytes 589824
  139.7 1.4 copy.20
  141.1 1.3 copy.21
  142.5 1.4 copy.22
  143.8 1.3 copy.23

commit v2 on v1

v2 whole, which is shorter than its diff:
```python
import jax
import jax.numpy as jnp
from jax import lax
from jax.experimental import pallas as pl
from jax.experimental.pallas import tpu as pltpu
from jax.sharding import PartitionSpec as P

F32 = jnp.float32
BF = jnp.bfloat16
MESH = pl.DeviceIdType.MESH
HD = 72
HEADS = 8
ATT = 576
D = 1152
QKV = 1728
EPS = 1e-06
SCALE = HD**-0.5


def nn(a, b):
    return lax.dot_general(a, b, (((1,), (0,)), ((), ())), preferred_element_type=F32)


def nt(a, b):
    return lax.dot_general(a, b, (((1,), (1,)), ((), ())), preferred_element_type=F32)


def tn(a, b):
    return lax.dot_general(a, b, (((0,), (0,)), ((), ())), preferred_element_type=F32)


def owner(c, h):
    return (h // 2) * 4 + c * 2 + h % 2


def normalise(x):
    centre = x - jnp.mean(x, axis=-1, keepdims=True)
    r = lax.rsqrt(jnp.mean(centre * centre, axis=-1, keepdims=True) + EPS)
    return centre * r, r


def normalise_back(dn, stretch, xh, r):
    dx = dn * (1.0 + stretch)
    dx = dx - xh * jnp.mean(dx * xh, axis=-1, keepdims=True)
    dx = r * dx
    return dx - jnp.mean(dx, axis=-1, keepdims=True)


def inverse_norm(x):
    return lax.rsqrt(jnp.sum(x * x, axis=-1, keepdims=True) * (1.0 / HD) + EPS)


def head_back(dy, y, r):
    return r * (dy - y * (jnp.sum(dy * y, axis=-1, keepdims=True) * (1.0 / HD)))


def rounded(x):
    return x.astype(BF).astype(F32)


def zeros(*shape):
    return jnp.zeros(shape, F32)


def fold(x, near):
    n, _, w = x.shape
    far = x[:, :, near:]
    pad = 2 * near - w
    far = jnp.concatenate([far, zeros(n, 8, pad)], axis=-1)
    return jnp.concatenate([x[:, :, :near], far], axis=1)


def unfold(x, w):
    near = x.shape[-1]
    return jnp.concatenate([x[:, :8, :], x[:, 8:, : w - near]], axis=-1)


def widen(x, width):
    return jnp.concatenate([x, zeros(x.shape[0], width - x.shape[1])], axis=-1)


class Exchange:
    def __init__(self, send, recv, ssem, rsem, n, me, place):
        self.send, self.recv, self.ssem, self.rsem = send, recv, ssem, rsem
        self.n, self.me, self.place = n, me, place

    def copy(self, to, slot):
        return pltpu.make_async_remote_copy(
            src_ref=self.send.at[to],
            dst_ref=self.recv.at[slot],
            send_sem=self.ssem.at[to],
            recv_sem=self.rsem.at[slot],
            device_id=self.place(to),
            device_id_type=MESH,
        )

    def start(self):
        def step(i, carry):
            self.copy(lax.rem(self.me + i, self.n), self.me).start()
            return carry

        lax.fori_loop(1, self.n, step, 0)
        self.recv[self.me] = self.send[self.me]

    def wait(self):
        def step(i, carry):
            other = lax.rem(self.me + self.n - i, self.n)
            self.copy(other, other).wait()
            return carry

        lax.fori_loop(1, self.n, step, 0)


def kernel(
    lat, cot, mod_s, mod_t, wqs_h, wos_h, wqt_h, wot_h,
    gl, gqs, gos, gqt, got,
    wqs, wos, wqt, wot, wsem,
    normed, proj,
    a_s, a_r, b1_s, b1_r, att_s, scaled, dmid, t1_s, t1_r, t2_s, t2_r,
    c2_s, c2_r, c1_s, c1_r, dm_s, dm_r, d_s, d_r, dg, ngt, xsems,
    q_b, k_b, v_b, rqk, do_b, kt_b, dq_f, dk_f, dv_f,
    ng, ngsem, xn, xnsem, dt_s, dt_r, dtsem,
    xl, xrv, xr, xsem, lt,
    syq, ryq, syo, ryo, sxo, rxo, sxs, rxs, sys, rys, gys, gyr, sem4,
    szq, rzq, szo, rzo, sem8,
    fs, fr, fs_sem, fr_sem,
):
    f = lax.axis_index("frame")
    p = lax.axis_index("patch")
    core = lax.rem(p, 2)
    zh = lax.rem(lax.div(p, 2), 2)
    x = lax.div(p, 4)
    y = lax.rem(f, 4)
    zl = lax.div(f, 4)
    head = 2 * x + core
    clip_t = lax.div(f, 8)
    z = zh * 4 + zl

    loads = [
        pltpu.make_async_copy(src, dst, wsem.at[i])
        for i, (src, dst) in enumerate(
            ((wqs_h, wqs), (wot_h, wot), (wos_h, wos), (wqt_h, wqt))
        )
    ]
    loads[0].start()

    barrier = pltpu.get_barrier_semaphore()

    def greet(i, carry):
        pl.semaphore_signal(
            barrier, inc=1, device_id={"frame": lax.rem(f + i, 16)}, device_id_type=MESH
        )
        pl.semaphore_signal(
            barrier, inc=1, device_id={"patch": lax.rem(p + i, 16)}, device_id_type=MESH
        )
        return carry

    lax.fori_loop(1, 16, greet, 0)

    def greet_far(i, carry):
        pl.semaphore_signal(
            barrier,
            inc=1,
            device_id={
                "frame": 4 * lax.rem(zl + 1 + lax.div(i, 15), 4) + y,
                "patch": lax.rem(p + 1 + lax.rem(i, 15), 16),
            },
            device_id_type=MESH,
        )
        return carry

    lax.fori_loop(0, 45, greet_far, 0)

    def on_patch(i):
        return {"patch": i}

    def on_frame(i):
        return {"frame": i}

    def on_x(i):
        return {"patch": 4 * i + 2 * zh + core}

    def on_y(i):
        return {"frame": 4 * zl + i}

    def on_column(i):
        return {"patch": 4 * lax.rem(i, 4) + 2 * zh + lax.div(i, 4)}

    def on_z(i):
        return {
            "frame": 4 * lax.rem(i, 4) + y,
            "patch": 4 * x + 2 * lax.div(i, 4) + core,
        }

    ex_a = Exchange(a_s, a_r, xsems.at[0, 0], xsems.at[0, 1], 16, p, on_patch)
    ex_b1 = Exchange(b1_s, b1_r, xsems.at[1, 0], xsems.at[1, 1], 16, p, on_patch)
    ex_t1 = Exchange(t1_s, t1_r, xsems.at[3, 0], xsems.at[3, 1], 16, f, on_frame)
    ex_t2 = Exchange(t2_s, t2_r, xsems.at[4, 0], xsems.at[4, 1], 16, f, on_frame)
    ex_c2 = Exchange(c2_s, c2_r, xsems.at[5, 0], xsems.at[5, 1], 16, f, on_frame)
    ex_c1 = Exchange(c1_s, c1_r, xsems.at[6, 0], xsems.at[6, 1], 16, p, on_patch)
    ex_dm = Exchange(dm_s, dm_r, xsems.at[7, 0], xsems.at[7, 1], 16, f, on_frame)
    ex_d = Exchange(d_s, d_r, xsems.at[8, 0], xsems.at[8, 1], 16, p, on_patch)
    ex_dt = Exchange(dt_s, dt_r, dtsem.at[0], dtsem.at[1], 8, 4 * core + x, on_column)
    ex_yq = Exchange(syq, ryq, sem4.at[0, 0], sem4.at[0, 1], 4, y, on_y)
    ex_yo = Exchange(syo, ryo, sem4.at[1, 0], sem4.at[1, 1], 4, y, on_y)
    ex_xo = Exchange(sxo, rxo, sem4.at[2, 0], sem4.at[2, 1], 4, x, on_x)
    ex_xs = Exchange(sxs, rxs, sem4.at[4, 0], sem4.at[4, 1], 4, x, on_x)
    ex_ys = Exchange(sys, rys, sem4.at[5, 0], sem4.at[5, 1], 4, y, on_y)
    ex_gy = Exchange(gys, gyr, sem4.at[3, 0], sem4.at[3, 1], 4, y, on_y)
    ex_zq = Exchange(szq, rzq, sem8.at[0, 0], sem8.at[0, 1], 8, z, on_z)
    ex_zo = Exchange(szo, rzo, sem8.at[1, 0], sem8.at[1, 1], 8, z, on_z)

    for c in range(2):
        xh, _ = normalise(lat[c].astype(F32))
        normed[c] = (xh * (1.0 + mod_s[1, c : c + 1, :]) + mod_s[0, c : c + 1, :]).astype(BF)
    loads[0].wait()
    for load in loads[1:]:
        load.start()
    proj[...] = nt(normed[...].reshape(128, D), wqs[...])
    lane = lax.broadcasted_iota(jnp.int32, (128, 224), 1)
    for h in range(HEADS):
        q = proj[:, HD * h : HD * h + HD]
        k = proj[:, ATT + HD * h : ATT + HD * h + HD]
        v = proj[:, 2 * ATT + HD * h : 2 * ATT + HD * h + HD]
        rq = inverse_norm(q)
        rk = inverse_norm(k)
        row = jnp.concatenate([q * rq, k * rk, v, zeros(128, 8)], axis=-1)
        row = jnp.where(lane == 216, rq, row)
        row = jnp.where(lane == 217, rq - rounded(rq), row)
        row = jnp.where(lane == 218, rk, row)
        row = jnp.where(lane == 219, rk - rounded(rk), row)
        row = row.reshape(2, 4, 16, 224)
        for c in range(2):
            quarters = [row[c, j] for j in range(4)]
            a_s[owner(c, h)] = jnp.concatenate(quarters, axis=-1).astype(BF)
    pl.semaphore_wait(barrier, 75)
    ex_a.start()

    loads[1].wait()
    for c in range(2):
        scaled[c] = (cot[c].astype(F32) * mod_t[2, c : c + 1, :]).astype(BF)
    dout = nt(scaled[...].reshape(128, D), wot[...])
    for c in range(2):
        part = dout[64 * c : 64 * c + 64].reshape(8, 8, ATT)
        t2_s[8 * c : 8 * c + 8] = fold(part, 384).astype(BF)
    ex_a.wait()
    ng[core, x, zh] = normed[zh]
    gather_z = pltpu.make_async_remote_copy(
        src_ref=normed.at[1 - zh],
        dst_ref=ng.at[core, x, zh],
        send_sem=ngsem.at[0, 0],
        recv_sem=ngsem.at[1, 0],
        device_id={"patch": 4 * x + 2 * (1 - zh) + core},
        device_id_type=MESH,
    )
    gather_z.start()

    for part in range(4):
        rows = a_r[4 * part : 4 * part + 4].astype(F32)
        rows = [rows[:, :, 224 * j : 224 * j + 224] for j in range(4)]
        rows = jnp.stack(rows, axis=1).reshape(256, 224)
        at = pl.ds(256 * part, 256)
        q_b[at, :] = rows[:, 0:HD].astype(BF)
        k_b[at, :] = rows[:, HD : 2 * HD].astype(BF)
        v_b[at, :] = rows[:, 2 * HD : 3 * HD].astype(BF)
        rqk[at, 0:1] = rows[:, 216:217] + rows[:, 217:218]
        rqk[at, 1:2] = rows[:, 218:219] + rows[:, 219:220]

    def attend(i, carry):
        part = lax.rem(x + 1 + i, 4)
        at = pl.ds(pl.multiple_of(part * 256, 256), 256)
        e = jnp.exp(nt(q_b[at, :], k_b[...]) * SCALE)
        weights = (e * (1.0 / jnp.sum(e, axis=-1, keepdims=True))).astype(BF)
        pieces = nn(weights, v_b[...]).reshape(4, 4, 16, HD)
        row = [pieces[:, j].reshape(64, HD) for j in range(4)] + [zeros(64, 96)]
        row = jnp.concatenate(row, axis=-1).astype(BF).reshape(4, 16, 384)
        b1_s[pl.ds(4 * part, 4)] = row
        for j in range(4):
            to = 4 * part + j

            @pl.when(to != p)
            def _():
                ex_b1.copy(to, p).start()

        return carry

    lax.fori_loop(0, 4, attend, 0)
    b1_r[p] = b1_s[p]
    ex_t2.start()
    loads[2].wait()
    ex_b1.wait()
    atts = []
    for c in range(2):
        blocks = [b1_r[owner(c, h)].astype(F32) for h in range(HEADS)]
        rows = [
            jnp.concatenate([b[:, HD * j : HD * j + HD] for b in blocks], axis=-1)
            for j in range(4)
        ]
        atts.append(jnp.concatenate(rows, axis=0))
    att_s[...] = jnp.concatenate(atts, axis=0).astype(BF)
    added = nn(att_s[...], wos[...])
    for c in range(2):
        middle = lat[c].astype(F32) + mod_s[2, c : c + 1, :] * added[64 * c : 64 * c + 64]
        t1_s[8 * c : 8 * c + 8] = fold(middle.reshape(8, 8, D), 640).astype(BF)
    ex_t1.start()

    gather_z.wait()

    def gather_x(i, back):
        block = lax.rem(x + 4 - i, 4) if back else x
        return pltpu.make_async_remote_copy(
            src_ref=ng.at[core, block],
            dst_ref=ng.at[core, block],
            send_sem=ngsem.at[0, i],
            recv_sem=ngsem.at[1, i],
            device_id=on_x(lax.rem(x + i, 4)),
            device_id_type=MESH,
        )

    def gather_core(back):
        side = 1 - core if back else core
        return pltpu.make_async_remote_copy(
            src_ref=ng.at[side],
            dst_ref=ng.at[side],
            send_sem=ngsem.at[0, 4],
            recv_sem=ngsem.at[1, 4],
            device_id={"patch": p + 1 - 2 * core},
            device_id_type=MESH,
        )

    for i in range(1, 4):
        gather_x(i, False).start()

    def pick(ref, i):
        return jnp.where(clip_t == 0, ref[i, 0:1, :], ref[i, 1:2, :])

    shift_t, stretch_t = pick(mod_t, 0), pick(mod_t, 1)

    def spread_rows(a):
        parts = []
        for yy in range(4):
            for zz in range(4):
                at = 36 * (4 * zz + yy)
                parts += [a[:, at : at + 36], zeros(128, 4)]
        return parts

    def core_columns(full, cc):
        parts = [full[:, HD * (2 * b + cc) : HD * (2 * b + cc) + HD] for b in range(8)]
        return jnp.concatenate(parts + [zeros(128, 64)], axis=-1).astype(BF)

    xl[core, :, 640:1280] = jnp.concatenate(
        spread_rows(att_s[...].astype(F32)), axis=-1
    ).astype(BF)
    for cc in range(2):
        xrv[cc, :, 0:640] = core_columns(scaled[...].reshape(128, D).astype(F32), cc)

    loads[3].wait()
    ex_t1.wait()
    middle = unfold(t1_r[...].astype(F32), D).reshape(128, D)
    xh_t, r_t = normalise(middle)
    normed_t = (xh_t * (1.0 + stretch_t) + shift_t).astype(BF)
    xn[4 * core + x] = normed_t

    def normed_x(i, back):
        block = 4 * core + (lax.rem(x + 4 - i, 4) if back else x)
        return pltpu.make_async_remote_copy(
            src_ref=xn.at[block],
            dst_ref=xn.at[block],
            send_sem=xnsem.at[0, i],
            recv_sem=xnsem.at[1, i],
            device_id=on_x(lax.rem(x + i, 4)),
            device_id_type=MESH,
        )

    def normed_core(back):
        side = pl.ds(4 * (1 - core if back else core), 4)
        return pltpu.make_async_remote_copy(
            src_ref=xn.at[side],
            dst_ref=xn.at[side],
            send_sem=xnsem.at[0, 0],
            recv_sem=xnsem.at[1, 0],
            device_id={"patch": p + 1 - 2 * core},
            device_id_type=MESH,
        )

    for i in range(1, 4):
        normed_x(i, False).start()
    proj[...] = nt(normed_t, wqt[...])
    ex_t2.wait()
    dout_t = unfold(t2_r[...].astype(F32), ATT).reshape(128, ATT)
    same = lax.rem(lax.broadcasted_iota(jnp.int32, (128, 128), 0), 8) == lax.rem(
        lax.broadcasted_iota(jnp.int32, (128, 128), 1), 8
    )
    att_parts, dq_parts, dk_parts, dv_parts = [], [], [], []
    for h in range(HEADS):
        q = proj[:, HD * h : HD * h + HD]
        k = proj[:, ATT + HD * h : ATT + HD * h + HD]
        v = proj[:, 2 * ATT + HD * h : 2 * ATT + HD * h + HD].astype(BF)
        rq = inverse_norm(q)
        rk = inverse_norm(k)
        q = q * rq
        k = k * rk
        qb, kb = q.astype(BF), k.astype(BF)
        e = jnp.where(same, jnp.exp(nt(qb, kb) * SCALE), 0.0)
        soft = e * (1.0 / jnp.sum(e, axis=-1, keepdims=True))
        soft_b = soft.astype(BF)
        att_parts.append(nn(soft_b, v))
        do = dout_t[:, HD * h : HD * h + HD].astype(BF)
        dp = nt(do, v)
        ds = (soft * (dp - jnp.sum(dp * soft, axis=-1, keepdims=True)) * SCALE).astype(BF)
        dq_parts.append(head_back(rounded(nn(ds, kb)), q, rq))
        dk_parts.append(head_back(rounded(tn(ds, qb)), k, rk))
        dv_parts.append(tn(soft_b, do))
    att_t = jnp.concatenate(att_parts, axis=-1)
    dproj_t = jnp.concatenate(dq_parts + dk_parts + dv_parts, axis=-1)
    dn = nn(dproj_t.astype(BF), wqt[...])
    back = normalise_back(dn, stretch_t, xh_t, r_t)
    dm_s[...] = fold(back.reshape(16, 8, D), 640).astype(BF)
    ex_dm.start()
    c2_s[...] = fold(att_t.reshape(16, 8, ATT), 384).astype(BF)

    for cc in range(2):
        for xx in range(4):
            at = 108 * (4 * xx + cc)
            row = [dproj_t[:, at : at + 108], zeros(128, 20)]
            row += [dproj_t[:, at + 216 : at + 324], zeros(128, 20)]
            dt_s[4 * cc + xx] = jnp.concatenate(row, axis=-1).astype(BF)
    ex_dt.start()
    ex_c2.start()

    for i in range(1, 4):
        gather_x(i, True).wait()
    gather_core(False).start()
    for i in range(1, 4):
        normed_x(i, True).wait()
    normed_core(False).start()
    gather_core(True).wait()
    for i in range(8):
        block = ng[i // 4, i % 4].reshape(128, D).astype(F32)
        ngt[:, 128 * i : 128 * i + 128] = jnp.transpose(block).astype(BF)

    ex_dm.wait()
    back = unfold(dm_r[...].astype(F32), D).reshape(2, 64, D)
    parts = []
    for c in range(2):
        total = rounded(cot[c].astype(F32) + back[c])
        dmid[c] = total.astype(BF)
        parts.append((total * mod_s[2, c : c + 1, :]).astype(BF))
    scaled_s = jnp.concatenate(parts, axis=0)
    tokens = nt(scaled_s, wos[...]).reshape(2, 64, ATT)
    for c in range(2):
        for h in range(HEADS):
            part = tokens[c][:, HD * h : HD * h + HD].reshape(4, 16, HD)
            row = jnp.concatenate([part[j] for j in range(4)] + [zeros(16, 96)], axis=-1)
            c1_s[owner(c, h)] = row.astype(BF)
    ex_c1.start()

    ex_c2.wait()
    att_t = unfold(c2_r[...].astype(F32), ATT).reshape(128, ATT)
    xl[core, :, 0:640] = jnp.concatenate(spread_rows(att_t), axis=-1).astype(BF)
    for cc in range(2):
        xrv[cc, :, 640:1280] = core_columns(scaled_s.astype(F32), cc)
    xr[core] = xrv[core]

    def pair_copies(slot):
        there = {"patch": p + 1 - 2 * core}
        return [
            pltpu.make_async_remote_copy(
                src_ref=src,
                dst_ref=dst.at[slot],
                send_sem=xsem.at[0, i],
                recv_sem=xsem.at[1, i],
                device_id=there,
                device_id_type=MESH,
            )
            for i, (src, dst) in enumerate(((xl.at[core], xl), (xrv.at[1 - core], xr)))
        ]

    for copy in pair_copies(core):
        copy.start()

    for part in range(4):
        at = pl.ds(256 * part, 256)
        kt_b[:, at] = jnp.transpose(widen(k_b[at, :].astype(F32), 128)).astype(BF)
    normed_core(True).wait()
    ex_dt.wait()
    g = tn(xn[...].reshape(1024, D), dt_r[...].reshape(1024, 256)).reshape(4, 4, HD, 256)
    for yy in range(4):
        syq[yy] = g[:, yy].reshape(288, 256).astype(BF)
    ex_yq.start()
    for copy in pair_copies(1 - core):
        copy.wait()
    left = xl[...].reshape(256, 1280)
    right = xr[...].reshape(256, 1280)
    lt[0:640, :] = jnp.transpose(left[:, 0:640].astype(F32)).astype(BF)
    lt[640:1280, :] = jnp.transpose(right[:, 640:1280].astype(F32)).astype(BF)
    g = nn(lt[0:640, :], right[:, 0:640])
    for yy in range(4):
        syo[yy] = g[160 * yy : 160 * yy + 160].astype(BF)
    ex_yo.start()
    g = nn(lt[640:1280, :], left[:, 640:1280])
    for i in range(4):
        sxs[i] = g[144 * i : 144 * i + 144].astype(BF)
    ex_xs.start()
    ex_c1.wait()
    got_do = c1_r[...].astype(F32)
    parts = [got_do[:, :, HD * j : HD * j + HD] for j in range(4)]
    do_b[...] = jnp.stack(parts, axis=1).reshape(1024, HD).astype(BF)
    dk_f[...] = jnp.zeros_like(dk_f)
    dv_f[...] = jnp.zeros_like(dv_f)

    def attend_back(i, carry):
        at = pl.ds(pl.multiple_of(i * 256, 256), 256)
        qb, dob = q_b[at, :], do_b[at, :]
        e = jnp.exp(nt(k_b[...], qb) * SCALE)
        soft = e * (1.0 / jnp.sum(e, axis=0, keepdims=True))
        dv_f[...] += nn(soft.astype(BF), dob)
        dp = nt(v_b[...], dob)
        ds = (soft * (dp - jnp.sum(dp * soft, axis=0, keepdims=True)) * SCALE).astype(BF)
        dk_f[...] += nn(ds, qb)
        dq_f[at, :] = jnp.transpose(nn(kt_b[...], ds))[:, :HD]
        return carry

    lax.fori_loop(0, 4, attend_back, 0)
    for part in range(4):
        at = pl.ds(256 * part, 256)
        dq = head_back(rounded(dq_f[at, :]), q_b[at, :].astype(F32), rqk[at, 0:1])
        dk = head_back(rounded(dk_f[at, :]), k_b[at, :].astype(F32), rqk[at, 1:2])
        row = jnp.concatenate([dq, dk, dv_f[at, :], zeros(256, 8)], axis=-1)
        dg[4 * part : 4 * part + 4] = row.astype(BF).reshape(4, 64, 224)
        row = row.reshape(4, 4, 16, 224)
        row = jnp.concatenate([row[:, j].reshape(64, 224) for j in range(4)], axis=-1)
        d_s[4 * part : 4 * part + 4] = row.astype(BF).reshape(4, 16, 896)
    ex_d.start()

    ex_yq.wait()
    total = sum(ryq[i].astype(F32) for i in range(4))
    for i in range(8):
        zz, s = i % 4, i // 4
        part = total[HD * zz : HD * zz + HD, 128 * s : 128 * s + 128]
        szq[i] = jnp.concatenate([part, zeros(8, 128)], axis=0).astype(BF)
    ex_zq.start()

    blocks = [dg[4 * xx + 2 * s + cc] for cc in range(2) for xx in range(4) for s in range(2)]
    g = nn(ngt[...], jnp.concatenate(blocks, axis=0)).reshape(4, 4, HD, 224)
    for yy in range(4):
        gys[yy] = g[:, yy].reshape(288, 224).astype(BF)
    ex_gy.start()

    ex_yo.wait()
    total = sum(ryo[i].astype(F32) for i in range(4))
    for i in range(4):
        sxo[i] = widen(total[:, 144 * i : 144 * i + 144], 256).astype(BF)
    ex_xo.start()
    ex_xs.wait()
    total = sum(rxs[i].astype(F32) for i in range(4))
    for i in range(4):
        sys[i] = widen(total[:, 160 * i : 160 * i + 160], 256).astype(BF)
    ex_ys.start()

    ex_gy.wait()
    total = sum(gyr[i].astype(F32) for i in range(4)).reshape(4, 3, 24, 224)
    for b in range(6):
        cols = [total[:, r, :, 36 * b : 36 * b + 36] for r in range(3)] + [zeros(4, 24, 20)]
        cols = jnp.concatenate(cols, axis=-1)
        fs[:, b] = jnp.concatenate([cols, zeros(4, 8, 128)], axis=1).astype(BF)

    def piece(i, b):
        to_z = lax.rem(zl + i, 4)
        block = 16 * (b // 2) + 2 * head + b % 2
        to, slot = lax.div(block, 3), lax.rem(block, 3)
        copy = pltpu.make_async_remote_copy(
            src_ref=fs.at[to_z, b],
            dst_ref=fr.at[slot, z],
            send_sem=fs_sem.at[to_z, b],
            recv_sem=fr_sem.at[slot, z],
            device_id={"frame": 4 * to_z + y, "patch": to},
            device_id_type=MESH,
        )
        return to, slot, copy

    for i in range(4):
        for b in range(6):
            to, slot, copy = piece(i, b)
            if i > 0:
                copy.start()
            else:

                @pl.when(to != p)
                def _():
                    copy.start()

                @pl.when(to == p)
                def _():
                    fr[slot, z] = fs[zl, b]

    ex_xo.wait()
    ex_ys.wait()
    total = sum(rxo[i].astype(F32) for i in range(4))
    other = sum(rys[i].astype(F32) for i in range(4))
    other = jnp.transpose(jnp.concatenate([other, zeros(112, 256)], axis=0))
    for i in range(8):
        zz, s = i % 4, i // 4
        rows, cols = slice(40 * zz, 40 * zz + 40), slice(HD * s, HD * s + HD)
        part = jnp.concatenate([total[rows, cols], other[rows, cols]], axis=0)
        szo[i] = widen(part, 128).astype(BF)
    ex_zo.start()

    ex_d.wait()
    parts = []
    for c in range(2):
        blocks = [d_r[owner(c, h)].astype(F32) for h in range(HEADS)]
        for i in range(4):
            at = [224 * i + HD * j for j in range(3)]
            row = [b[:, a : a + HD] for a in at for b in blocks]
            parts.append(jnp.concatenate(row, axis=-1))
    dn = nn(jnp.concatenate(parts, axis=0).astype(BF), wqs[...])
    for c in range(2):
        xh, r = normalise(lat[c].astype(F32))
        back = normalise_back(dn[64 * c : 64 * c + 64], mod_s[1, c : c + 1, :], xh, r)
        gl[c] = (dmid[c].astype(F32) + back).astype(BF)


    ex_zq.wait()
    total = sum(rzq[i].astype(F32) for i in range(8))
    gqt[...] = total[:HD, :108]
    ex_zo.wait()
    total = sum(rzo[i].astype(F32) for i in range(8))
    got[...] = total[:36, :HD]
    gos[...] = total[40:76, :HD]

    for i in range(4):
        for b in range(6):
            to, slot, copy = piece(i, b)
            if i > 0:
                copy.wait_send()
            else:

                @pl.when(to != p)
                def _():
                    copy.wait_send()

    for slot in range(3):
        left = lax.rem(3 * p + slot, 16)
        source = lax.div(left, 4) * 4 + lax.rem(lax.div(left, 2), 2)
        for i in range(4):
            for c in range(2):
                from_z = lax.rem(zl + i, 4)
                at = 4 * c + from_z
                copy = pltpu.make_async_remote_copy(
                    src_ref=fs.at[0, 0],
                    dst_ref=fr.at[slot, at],
                    send_sem=fs_sem.at[0, 0],
                    recv_sem=fr_sem.at[slot, at],
                    device_id={"frame": 4 * from_z + y, "patch": source + 2 * c},
                    device_id_type=MESH,
                )
                if i > 0:
                    copy.wait_recv()
                else:

                    @pl.when(source + 2 * c != p)
                    def _():
                        copy.wait_recv()

    cols = []
    for slot in range(3):
        total = sum(fr[slot, i].astype(F32) for i in range(8))
        cols.append(
            jnp.concatenate([total[:24, 36 * r : 36 * r + 36] for r in range(3)], axis=0)
        )
    gqs[...] = jnp.concatenate(cols, axis=-1)


def hand_over(*refs):
    for src, dst in zip(refs[:5], refs[5:]):
        dst[...] = src[...]


def body(lat, mod_s, mod_t, wqs, wos, wqt, wot, cot):
    vmem = pl.BlockSpec(memory_space=pltpu.VMEM)
    hbm = pl.BlockSpec(memory_space=pl.ANY)
    dma = pltpu.SemaphoreType.DMA

    def buf(*shape):
        return pltpu.VMEM(shape, BF)

    def wide(*shape):
        return pltpu.VMEM(shape, F32)

    outs = pl.pallas_call(
        kernel,
        out_shape=(
            jax.ShapeDtypeStruct((2, 64, D), BF),
            jax.ShapeDtypeStruct((72, 108), F32),
            jax.ShapeDtypeStruct((36, 72), F32),
            jax.ShapeDtypeStruct((72, 108), F32),
            jax.ShapeDtypeStruct((36, 72), F32),
        ),
        in_specs=[vmem] * 4 + [hbm] * 4,
        out_specs=(vmem,) * 5,
        scratch_shapes=[
            buf(QKV, D), buf(ATT, D), buf(QKV, D), buf(ATT, D), dma((4,)),
            buf(2, 64, D), wide(128, QKV),
            buf(16, 16, 896), buf(16, 16, 896),
            buf(16, 16, 384), buf(16, 16, 384),
            buf(128, ATT), buf(2, 64, D), buf(2, 64, D),
            buf(16, 16, 640), buf(16, 16, 640),
            buf(16, 16, 384), buf(16, 16, 384),
            buf(16, 16, 384), buf(16, 16, 384),
            buf(16, 16, 384), buf(16, 16, 384),
            buf(16, 16, 640), buf(16, 16, 640),
            buf(16, 16, 896), buf(16, 16, 896), buf(16, 64, 224), buf(1152, 1024),
            dma((9, 2, 16)),
            buf(1024, HD), buf(1024, HD), buf(1024, HD), wide(1024, 2),
            buf(1024, HD), buf(128, 1024), wide(1024, HD), wide(1024, HD), wide(1024, HD),
            buf(2, 4, 2, 64, D), dma((2, 5)),
            buf(8, 128, D), dma((2, 4)), buf(8, 128, 256), buf(8, 128, 256), dma((2, 8)),
            buf(2, 128, 1280), buf(2, 128, 1280), buf(2, 128, 1280), dma((2, 2)),
            buf(1280, 256),
            buf(4, 288, 256), buf(4, 288, 256),
            buf(4, 160, 640), buf(4, 160, 640),
            buf(4, 160, 256), buf(4, 160, 256),
            buf(4, 144, 640), buf(4, 144, 640),
            buf(4, 144, 256), buf(4, 144, 256),
            buf(4, 288, 224), buf(4, 288, 224),
            dma((6, 2, 4)),
            buf(8, 80, 128), buf(8, 80, 128),
            buf(8, 80, 128), buf(8, 80, 128),
            dma((2, 2, 8)),
            buf(4, 6, 32, 128), buf(3, 8, 32, 128), dma((4, 6)), dma((3, 8)),
        ],
        compiler_params=pltpu.CompilerParams(
            collective_id=0, has_side_effects=True, vmem_limit_bytes=60 * 1024 * 1024
        ),
    )(
        lat.reshape(2, 64, D),
        cot.reshape(2, 64, D),
        mod_s.transpose(1, 0, 2),
        mod_t.transpose(1, 0, 2),
        wqs.T,
        wos,
        wqt.T,
        wot,
    )
    outs = pl.pallas_call(
        hand_over,
        out_shape=tuple(jax.ShapeDtypeStruct(o.shape, o.dtype) for o in outs),
        in_specs=[vmem] * 5,
        out_specs=(vmem,) * 5,
    )(*outs)
    return (outs[0].reshape(2, 1, 64, D),) + tuple(outs[1:])


def solution(mesh):
    tokens = P(None, "frame", "patch", None)
    return jax.shard_map(
        body,
        mesh=mesh,
        in_specs=(tokens,) + (P(),) * 6 + (tokens,),
        out_specs=(tokens,) + (P("frame", "patch"),) * 4,
        check_vma=False,
    )
```

time: 147 us -> 119 us (0.81); the launches traced: 145 us -> 119 us
  Pallas kernels: 137 us -> 118 us
  local copies, waits for them, and re-layouts: 7.14 us -> 0 us
    pallas_call x1, Pallas kernels: 137 us -> 116 us  [body(): pl.pallas_call(kernel, out_shape=(jax.ShapeDtypeStruct((2, 64, D), BF), j...]
    unnamed x5 -> x0, local copies, waits for them, and re-layouts: 7.14 us -> none
    pallas_call x0 -> x1, Pallas kernels: none -> 1.76 us  [body(): pl.pallas_call(hand_over, out_shape=tuple((jax.ShapeDtypeStruct(o.shape,...]
where the time goes in v2:
time: 119 us
  Pallas kernels  118 us (99%)
    pallas_call x1, Pallas kernels, body(): pl.pallas_call(kernel, out_shape=(jax.ShapeDtypeStruct((2, 64, D), BF), j...  116 us

profile of v2, /device:TPU:32, one launch (start us, length us, event | category | flops | bytes accessed | tf_op | source)
XLA Modules:
  0.0 118.8 jit_solution(17863348779557653876)
XLA Ops:
  0.6 116.4 %shard_map.119 = (bf16[2,64,1152]{2,1,0:T(8,128)(2,1)}, f32[72,108]{1,0:T(8,128)}, f32[36,72]{1,0:T(8,128)}, f32[72,108]{1,0:T(8,128)}, f32[36,72]{1,0:T(8,128)}) custom-call(bf16[2,64,1152]{2,1,0:T(8,128)(2,1)} %bitcast.11, bf16[2,64,1152]{2,1,0:T(8,128)(2,1)} %bitcast.12, f32[3,2,1152]{2,1,0:T(2,128)} %bitcast.13, f32[3,2,1152]{2,1,0:T(2,128)} %bitcast.14, ...), custom_call_target="tpu_custom_call" | custom-call | tf_op jit(solution)/shard_map/pallas_call | solution.py:691
  117.0 1.8 %shard_map.120 = (bf16[2,64,1152]{2,1,0:T(8,128)(2,1)}, f32[72,108]{1,0:T(8,128)}, f32[36,72]{1,0:T(8,128)}, f32[72,108]{1,0:T(8,128)}, f32[36,72]{1,0:T(8,128)}) custom-call(bf16[2,64,1152]{2,1,0:T(8,128)(2,1)} %get-tuple-element.15.refs_0_, f32[72,108]{1,0:T(8,128)} %get-tuple-element.16.refs_1_, f32[36,72]{1,0:T(8,128)} %get-tuple-element.17.refs_2_, ...), custom_call_target="tpu_custom_call" | custom-call | tf_op jit(solution)/shard_map/pallas_call | solution.py:746

commit v3 on v2

--- a/solution.py
+++ b/solution.py
@@ -15,6 +15,7 @@
 QKV = 1728
 EPS = 1e-06
 SCALE = HD**-0.5
+LOG2E = 1.4426950408889634
 
 
 def nn(a, b):
@@ -88,8 +89,8 @@
         return pltpu.make_async_remote_copy(
             src_ref=self.send.at[to],
             dst_ref=self.recv.at[slot],
-            send_sem=self.ssem.at[to],
-            recv_sem=self.rsem.at[slot],
+            send_sem=self.ssem,
+            recv_sem=self.rsem,
             device_id=self.place(to),
             device_id_type=MESH,
         )
@@ -103,22 +104,20 @@
         self.recv[self.me] = self.send[self.me]
 
     def wait(self):
-        def step(i, carry):
-            other = lax.rem(self.me + self.n - i, self.n)
-            self.copy(other, other).wait()
-            return carry
-
-        lax.fori_loop(1, self.n, step, 0)
+        for ref, sem in ((self.send, self.ssem), (self.recv, self.rsem)):
+            blocks = ref.at[pl.ds(0, self.n - 1)]
+            pltpu.make_async_copy(blocks, blocks, sem).wait()
 
 
 def kernel(
-    lat, cot, mod_s, mod_t, wqs_h, wos_h, wqt_h, wot_h,
-    gl, gqs, gos, gqt, got,
+    lat_h, cot_h, mod_s_h, mod_t_h, wqs_h, wos_h, wqt_h, wot_h,
+    gl_h, gqs_h, gos_h, gqt_h, got_h,
+    lat, cot, mod_s, mod_t, gl, gqs, gos, gqt, got, iosem,
     wqs, wos, wqt, wot, wsem,
     normed, proj,
     a_s, a_r, b1_s, b1_r, att_s, scaled, dmid, t1_s, t1_r, t2_s, t2_r,
     c2_s, c2_r, c1_s, c1_r, dm_s, dm_r, d_s, d_r, dg, ngt, xsems,
-    q_b, k_b, v_b, rqk, do_b, kt_b, dq_f, dk_f, dv_f,
+    q_b, k_b, v_b, rqk, rl, rrow, do_b, kt_b, dq_f, dk_f, dv_f,
     ng, ngsem, xn, xnsem, dt_s, dt_r, dtsem,
     xl, xrv, xr, xsem, lt,
     syq, ryq, syo, ryo, sxo, rxo, sxs, rxs, sys, rys, gys, gyr, sem4,
@@ -142,7 +141,23 @@
             ((wqs_h, wqs), (wot_h, wot), (wos_h, wos), (wqt_h, wqt))
         )
     ]
+    reads = [
+        pltpu.make_async_copy(src, dst, iosem.at[i])
+        for i, (src, dst) in enumerate(
+            ((lat_h, lat), (mod_s_h, mod_s), (cot_h, cot), (mod_t_h, mod_t))
+        )
+    ]
+    writes = [
+        pltpu.make_async_copy(src, dst, iosem.at[4 + i])
+        for i, (src, dst) in enumerate(
+            ((gl, gl_h), (gqt, gqt_h), (got, got_h), (gos, gos_h), (gqs, gqs_h))
+        )
+    ]
+    for read in reads[:2]:
+        read.start()
     loads[0].start()
+    for read in reads[2:]:
+        read.start()
 
     barrier = pltpu.get_barrier_semaphore()
 
@@ -210,6 +225,8 @@
     ex_zq = Exchange(szq, rzq, sem8.at[0, 0], sem8.at[0, 1], 8, z, on_z)
     ex_zo = Exchange(szo, rzo, sem8.at[1, 0], sem8.at[1, 1], 8, z, on_z)
 
+    reads[0].wait()
+    reads[1].wait()
     for c in range(2):
         xh, _ = normalise(lat[c].astype(F32))
         normed[c] = (xh * (1.0 + mod_s[1, c : c + 1, :]) + mod_s[0, c : c + 1, :]).astype(BF)
@@ -236,6 +253,8 @@
     pl.semaphore_wait(barrier, 75)
     ex_a.start()
 
+    reads[2].wait()
+    reads[3].wait()
     loads[1].wait()
     for c in range(2):
         scaled[c] = (cot[c].astype(F32) * mod_t[2, c : c + 1, :]).astype(BF)
@@ -243,7 +262,6 @@
     for c in range(2):
         part = dout[64 * c : 64 * c + 64].reshape(8, 8, ATT)
         t2_s[8 * c : 8 * c + 8] = fold(part, 384).astype(BF)
-    ex_a.wait()
     ng[core, x, zh] = normed[zh]
     gather_z = pltpu.make_async_remote_copy(
         src_ref=normed.at[1 - zh],
@@ -253,6 +271,7 @@
         device_id={"patch": 4 * x + 2 * (1 - zh) + core},
         device_id_type=MESH,
     )
+    ex_a.wait()
     gather_z.start()
 
     for part in range(4):
@@ -269,9 +288,10 @@
     def attend(i, carry):
         part = lax.rem(x + 1 + i, 4)
         at = pl.ds(pl.multiple_of(part * 256, 256), 256)
-        e = jnp.exp(nt(q_b[at, :], k_b[...]) * SCALE)
-        weights = (e * (1.0 / jnp.sum(e, axis=-1, keepdims=True))).astype(BF)
-        pieces = nn(weights, v_b[...]).reshape(4, 4, 16, HD)
+        e = jnp.exp2(nt(q_b[at, :], k_b[...]) * (SCALE * LOG2E))
+        r = 1.0 / jnp.sum(e, axis=-1, keepdims=True)
+        rl[at, :] = r
+        pieces = (nn(e.astype(BF), v_b[...]) * r).reshape(4, 4, 16, HD)
         row = [pieces[:, j].reshape(64, HD) for j in range(4)] + [zeros(64, 96)]
         row = jnp.concatenate(row, axis=-1).astype(BF).reshape(4, 16, 384)
         b1_s[pl.ds(4 * part, 4)] = row
@@ -287,6 +307,9 @@
     lax.fori_loop(0, 4, attend, 0)
     b1_r[p] = b1_s[p]
     ex_t2.start()
+    for part in range(4):
+        at = pl.ds(256 * part, 256)
+        rrow[:, at] = jnp.transpose(widen(rl[at, :], 128))[0:1, :]
     loads[2].wait()
     ex_b1.wait()
     atts = []
@@ -348,12 +371,29 @@
         parts = [full[:, HD * (2 * b + cc) : HD * (2 * b + cc) + HD] for b in range(8)]
         return jnp.concatenate(parts + [zeros(128, 64)], axis=-1).astype(BF)
 
-    xl[core, :, 640:1280] = jnp.concatenate(
-        spread_rows(att_s[...].astype(F32)), axis=-1
-    ).astype(BF)
+    xl[1, core] = jnp.concatenate(spread_rows(att_s[...].astype(F32)), axis=-1).astype(BF)
     for cc in range(2):
-        xrv[cc, :, 0:640] = core_columns(scaled[...].reshape(128, D).astype(F32), cc)
-
+        xrv[0, cc] = core_columns(scaled[...].reshape(128, D).astype(F32), cc)
+    xr[0, core] = xrv[0, core]
+
+    def pair_copies(which, slot):
+        there = {"patch": p + 1 - 2 * core}
+        pairs = ((xl.at[which, core], xl), (xrv.at[which, 1 - core], xr))
+        return [
+            pltpu.make_async_remote_copy(
+                src_ref=src,
+                dst_ref=dst.at[which, slot],
+                send_sem=xsem.at[0, 2 * which + i],
+                recv_sem=xsem.at[1, 2 * which + i],
+                device_id=there,
+                device_id_type=MESH,
+            )
+            for i, (src, dst) in enumerate(pairs)
+        ]
+
+    for part in range(4):
+        at = pl.ds(256 * part, 256)
+        kt_b[:, at] = jnp.transpose(widen(k_b[at, :].astype(F32), 128)).astype(BF)
     loads[3].wait()
     ex_t1.wait()
     middle = unfold(t1_r[...].astype(F32), D).reshape(128, D)
@@ -386,12 +426,10 @@
     for i in range(1, 4):
         normed_x(i, False).start()
     proj[...] = nt(normed_t, wqt[...])
-    ex_t2.wait()
-    dout_t = unfold(t2_r[...].astype(F32), ATT).reshape(128, ATT)
     same = lax.rem(lax.broadcasted_iota(jnp.int32, (128, 128), 0), 8) == lax.rem(
         lax.broadcasted_iota(jnp.int32, (128, 128), 1), 8
     )
-    att_parts, dq_parts, dk_parts, dv_parts = [], [], [], []
+    heads, att_parts, dq_parts, dk_parts, dv_parts = [], [], [], [], []
     for h in range(HEADS):
         q = proj[:, HD * h : HD * h + HD]
         k = proj[:, ATT + HD * h : ATT + HD * h + HD]
@@ -400,24 +438,27 @@
         rk = inverse_norm(k)
         q = q * rq
         k = k * rk
-        qb, kb = q.astype(BF), k.astype(BF)
-        e = jnp.where(same, jnp.exp(nt(qb, kb) * SCALE), 0.0)
+        e = jnp.where(same, jnp.exp(nt(q.astype(BF), k.astype(BF)) * SCALE), 0.0)
         soft = e * (1.0 / jnp.sum(e, axis=-1, keepdims=True))
-        soft_b = soft.astype(BF)
-        att_parts.append(nn(soft_b, v))
+        att_parts.append(nn(soft.astype(BF), v))
+        heads.append((q, k, v, rq, rk, soft))
+    att_t = jnp.concatenate(att_parts, axis=-1)
+    c2_s[...] = fold(att_t.reshape(16, 8, ATT), 384).astype(BF)
+    ex_c2.start()
+    ex_t2.wait()
+    dout_t = unfold(t2_r[...].astype(F32), ATT).reshape(128, ATT)
+    for h, (q, k, v, rq, rk, soft) in enumerate(heads):
         do = dout_t[:, HD * h : HD * h + HD].astype(BF)
         dp = nt(do, v)
         ds = (soft * (dp - jnp.sum(dp * soft, axis=-1, keepdims=True)) * SCALE).astype(BF)
-        dq_parts.append(head_back(rounded(nn(ds, kb)), q, rq))
-        dk_parts.append(head_back(rounded(tn(ds, qb)), k, rk))
-        dv_parts.append(tn(soft_b, do))
-    att_t = jnp.concatenate(att_parts, axis=-1)
+        dq_parts.append(head_back(rounded(nn(ds, k.astype(BF))), q, rq))
+        dk_parts.append(head_back(rounded(tn(ds, q.astype(BF))), k, rk))
+        dv_parts.append(tn(soft.astype(BF), do))
     dproj_t = jnp.concatenate(dq_parts + dk_parts + dv_parts, axis=-1)
     dn = nn(dproj_t.astype(BF), wqt[...])
     back = normalise_back(dn, stretch_t, xh_t, r_t)
     dm_s[...] = fold(back.reshape(16, 8, D), 640).astype(BF)
     ex_dm.start()
-    c2_s[...] = fold(att_t.reshape(16, 8, ATT), 384).astype(BF)
 
     for cc in range(2):
         for xx in range(4):
@@ -426,14 +467,22 @@
             row += [dproj_t[:, at + 216 : at + 324], zeros(128, 20)]
             dt_s[4 * cc + xx] = jnp.concatenate(row, axis=-1).astype(BF)
     ex_dt.start()
-    ex_c2.start()
-
+
+    ex_c2.wait()
+    att_t = unfold(c2_r[...].astype(F32), ATT).reshape(128, ATT)
+    xl[0, core] = jnp.concatenate(spread_rows(att_t), axis=-1).astype(BF)
+    for copy in pair_copies(0, core):
+        copy.start()
     for i in range(1, 4):
         gather_x(i, True).wait()
     gather_core(False).start()
-    for i in range(1, 4):
-        normed_x(i, True).wait()
-    normed_core(False).start()
+    for copy in pair_copies(0, 1 - core):
+        copy.wait()
+    lt[...] = jnp.transpose(xl[0].reshape(256, 640).astype(F32)).astype(BF)
+    g = nn(lt[...], xr[0].reshape(256, 640))
+    for yy in range(4):
+        syo[yy] = g[160 * yy : 160 * yy + 160].astype(BF)
+    ex_yo.start()
     gather_core(True).wait()
     for i in range(8):
         block = ng[i // 4, i % 4].reshape(128, D).astype(F32)
@@ -455,68 +504,47 @@
             c1_s[owner(c, h)] = row.astype(BF)
     ex_c1.start()
 
-    ex_c2.wait()
-    att_t = unfold(c2_r[...].astype(F32), ATT).reshape(128, ATT)
-    xl[core, :, 0:640] = jnp.concatenate(spread_rows(att_t), axis=-1).astype(BF)
     for cc in range(2):
-        xrv[cc, :, 640:1280] = core_columns(scaled_s.astype(F32), cc)
-    xr[core] = xrv[core]
-
-    def pair_copies(slot):
-        there = {"patch": p + 1 - 2 * core}
-        return [
-            pltpu.make_async_remote_copy(
-                src_ref=src,
-                dst_ref=dst.at[slot],
-                send_sem=xsem.at[0, i],
-                recv_sem=xsem.at[1, i],
-                device_id=there,
-                device_id_type=MESH,
-            )
-            for i, (src, dst) in enumerate(((xl.at[core], xl), (xrv.at[1 - core], xr)))
-        ]
-
-    for copy in pair_copies(core):
+        xrv[1, cc] = core_columns(scaled_s.astype(F32), cc)
+    xr[1, core] = xrv[1, core]
+    for copy in pair_copies(1, core):
         copy.start()
-
-    for part in range(4):
-        at = pl.ds(256 * part, 256)
-        kt_b[:, at] = jnp.transpose(widen(k_b[at, :].astype(F32), 128)).astype(BF)
+    for i in range(1, 4):
+        normed_x(i, True).wait()
+    normed_core(False).start()
+    for copy in pair_copies(1, 1 - core):
+        copy.wait()
+    lt[...] = jnp.transpose(xr[1].reshape(256, 640).astype(F32)).astype(BF)
+    g = nn(lt[...], xl[1].reshape(256, 640))
+    for i in range(4):
+        sxs[i] = g[144 * i : 144 * i + 144].astype(BF)
+    ex_xs.start()
     normed_core(True).wait()
     ex_dt.wait()
     g = tn(xn[...].reshape(1024, D), dt_r[...].reshape(1024, 256)).reshape(4, 4, HD, 256)
     for yy in range(4):
         syq[yy] = g[:, yy].reshape(288, 256).astype(BF)
     ex_yq.start()
-    for copy in pair_copies(1 - core):
-        copy.wait()
-    left = xl[...].reshape(256, 1280)
-    right = xr[...].reshape(256, 1280)
-    lt[0:640, :] = jnp.transpose(left[:, 0:640].astype(F32)).astype(BF)
-    lt[640:1280, :] = jnp.transpose(right[:, 640:1280].astype(F32)).astype(BF)
-    g = nn(lt[0:640, :], right[:, 0:640])
-    for yy in range(4):
-        syo[yy] = g[160 * yy : 160 * yy + 160].astype(BF)
-    ex_yo.start()
-    g = nn(lt[640:1280, :], left[:, 640:1280])
+    ex_yo.wait()
+    total = sum(ryo[i].astype(F32) for i in range(4))
     for i in range(4):
-        sxs[i] = g[144 * i : 144 * i + 144].astype(BF)
-    ex_xs.start()
+        sxo[i] = widen(total[:, 144 * i : 144 * i + 144], 256).astype(BF)
+    ex_xo.start()
     ex_c1.wait()
     got_do = c1_r[...].astype(F32)
     parts = [got_do[:, :, HD * j : HD * j + HD] for j in range(4)]
-    do_b[...] = jnp.stack(parts, axis=1).reshape(1024, HD).astype(BF)
+    do_b[...] = (jnp.stack(parts, axis=1).reshape(1024, HD) * rl[...]).astype(BF)
     dk_f[...] = jnp.zeros_like(dk_f)
     dv_f[...] = jnp.zeros_like(dv_f)
 
     def attend_back(i, carry):
         at = pl.ds(pl.multiple_of(i * 256, 256), 256)
         qb, dob = q_b[at, :], do_b[at, :]
-        e = jnp.exp(nt(k_b[...], qb) * SCALE)
-        soft = e * (1.0 / jnp.sum(e, axis=0, keepdims=True))
-        dv_f[...] += nn(soft.astype(BF), dob)
+        e = jnp.exp2(nt(k_b[...], qb) * (SCALE * LOG2E))
         dp = nt(v_b[...], dob)
-        ds = (soft * (dp - jnp.sum(dp * soft, axis=0, keepdims=True)) * SCALE).astype(BF)
+        shift = rrow[:, at] * jnp.sum(dp * e, axis=0, keepdims=True)
+        ds = (e * (dp - shift)).astype(BF)
+        dv_f[...] += nn(e.astype(BF), dob)
         dk_f[...] += nn(ds, qb)
         dq_f[at, :] = jnp.transpose(nn(kt_b[...], ds))[:, :HD]
         return carry
@@ -524,39 +552,48 @@
     lax.fori_loop(0, 4, attend_back, 0)
     for part in range(4):
         at = pl.ds(256 * part, 256)
-        dq = head_back(rounded(dq_f[at, :]), q_b[at, :].astype(F32), rqk[at, 0:1])
-        dk = head_back(rounded(dk_f[at, :]), k_b[at, :].astype(F32), rqk[at, 1:2])
+        dq = head_back(rounded(dq_f[at, :] * SCALE), q_b[at, :].astype(F32), rqk[at, 0:1])
+        dk = head_back(rounded(dk_f[at, :] * SCALE), k_b[at, :].astype(F32), rqk[at, 1:2])
         row = jnp.concatenate([dq, dk, dv_f[at, :], zeros(256, 8)], axis=-1)
         dg[4 * part : 4 * part + 4] = row.astype(BF).reshape(4, 64, 224)
         row = row.reshape(4, 4, 16, 224)
         row = jnp.concatenate([row[:, j].reshape(64, 224) for j in range(4)], axis=-1)
         d_s[4 * part : 4 * part + 4] = row.astype(BF).reshape(4, 16, 896)
     ex_d.start()
-
-    ex_yq.wait()
-    total = sum(ryq[i].astype(F32) for i in range(4))
-    for i in range(8):
-        zz, s = i % 4, i // 4
-        part = total[HD * zz : HD * zz + HD, 128 * s : 128 * s + 128]
-        szq[i] = jnp.concatenate([part, zeros(8, 128)], axis=0).astype(BF)
-    ex_zq.start()
+    ex_xs.wait()
+    total = sum(rxs[i].astype(F32) for i in range(4))
+    for i in range(4):
+        sys[i] = widen(total[:, 160 * i : 160 * i + 160], 256).astype(BF)
+    ex_ys.start()
 
     blocks = [dg[4 * xx + 2 * s + cc] for cc in range(2) for xx in range(4) for s in range(2)]
     g = nn(ngt[...], jnp.concatenate(blocks, axis=0)).reshape(4, 4, HD, 224)
     for yy in range(4):
         gys[yy] = g[:, yy].reshape(288, 224).astype(BF)
     ex_gy.start()
-
-    ex_yo.wait()
-    total = sum(ryo[i].astype(F32) for i in range(4))
-    for i in range(4):
-        sxo[i] = widen(total[:, 144 * i : 144 * i + 144], 256).astype(BF)
-    ex_xo.start()
-    ex_xs.wait()
-    total = sum(rxs[i].astype(F32) for i in range(4))
-    for i in range(4):
-        sys[i] = widen(total[:, 160 * i : 160 * i + 160], 256).astype(BF)
-    ex_ys.start()
+    ex_yq.wait()
+    total = sum(ryq[i].astype(F32) for i in range(4))
+    for i in range(8):
+        zz, s = i % 4, i // 4
+        part = total[HD * zz : HD * zz + HD, 128 * s : 128 * s + 108]
+        rest = [part[64:, 18 * j : 18 * j + 18] for j in range(6)] + [zeros(16, 18)]
+        rest = jnp.concatenate(rest, axis=0)
+        szq[i] = jnp.concatenate([part[:64], rest, zeros(64, 2)], axis=-1).astype(BF)
+    ex_zq.start()
+
+
+    ex_xo.wait()
+    ex_ys.wait()
+    total = sum(rxo[i].astype(F32) for i in range(4))
+    other = sum(rys[i].astype(F32) for i in range(4))
+    other = jnp.transpose(jnp.concatenate([other, zeros(112, 256)], axis=0))
+    for i in range(8):
+        zz, s = i % 4, i // 4
+        rows, cols = slice(40 * zz, 40 * zz + 36), slice(HD * s, HD * s + HD)
+        part = jnp.concatenate([total[rows, cols], other[rows, cols]], axis=0)
+        rest = jnp.concatenate([part[48:, :36], part[48:, 36:]], axis=0)
+        szo[i] = jnp.concatenate([part[:48], rest, zeros(48, 20)], axis=-1).astype(BF)
+    ex_zo.start()
 
     ex_gy.wait()
     total = sum(gyr[i].astype(F32) for i in range(4)).reshape(4, 3, 24, 224)
@@ -572,8 +609,8 @@
         copy = pltpu.make_async_remote_copy(
             src_ref=fs.at[to_z, b],
             dst_ref=fr.at[slot, z],
-            send_sem=fs_sem.at[to_z, b],
-            recv_sem=fr_sem.at[slot, z],
+            send_sem=fs_sem.at[b if i == 0 else 6],
+            recv_sem=fr_sem.at[2 * slot + zh if i == 0 else 6],
             device_id={"frame": 4 * to_z + y, "patch": to},
             device_id_type=MESH,
         )
@@ -594,18 +631,6 @@
                 def _():
                     fr[slot, z] = fs[zl, b]
 
-    ex_xo.wait()
-    ex_ys.wait()
-    total = sum(rxo[i].astype(F32) for i in range(4))
-    other = sum(rys[i].astype(F32) for i in range(4))
-    other = jnp.transpose(jnp.concatenate([other, zeros(112, 256)], axis=0))
-    for i in range(8):
-        zz, s = i % 4, i // 4
-        rows, cols = slice(40 * zz, 40 * zz + 40), slice(HD * s, HD * s + HD)
-        part = jnp.concatenate([total[rows, cols], other[rows, cols]], axis=0)
-        szo[i] = widen(part, 128).astype(BF)
-    ex_zo.start()
-
     ex_d.wait()
     parts = []
     for c in range(2):
@@ -619,49 +644,51 @@
         xh, r = normalise(lat[c].astype(F32))
         back = normalise_back(dn[64 * c : 64 * c + 64], mod_s[1, c : c + 1, :], xh, r)
         gl[c] = (dmid[c].astype(F32) + back).astype(BF)
+    writes[0].start()
 
 
     ex_zq.wait()
     total = sum(rzq[i].astype(F32) for i in range(8))
-    gqt[...] = total[:HD, :108]
+    rest = [total[8 * j : 8 * j + 8, 108:126] for j in range(6)]
+    rest = jnp.concatenate(rest, axis=-1)
+    gqt[...] = jnp.concatenate([total[:, :108], rest], axis=0)
+    writes[1].start()
     ex_zo.wait()
     total = sum(rzo[i].astype(F32) for i in range(8))
-    got[...] = total[:36, :HD]
-    gos[...] = total[40:76, :HD]
-
-    for i in range(4):
-        for b in range(6):
-            to, slot, copy = piece(i, b)
-            if i > 0:
-                copy.wait_send()
-            else:
-
-                @pl.when(to != p)
-                def _():
-                    copy.wait_send()
+    rest = jnp.concatenate([total[:24, 72:108], total[24:, 72:108]], axis=-1)
+    total = jnp.concatenate([total[:, :HD], rest], axis=0)
+    got[...] = total[:36]
+    gos[...] = total[36:]
+    writes[2].start()
+    writes[3].start()
+
+    for b in range(6):
+        to, slot, copy = piece(0, b)
+
+        @pl.when(to != p)
+        def _():
+            copy.wait_send()
 
     for slot in range(3):
         left = lax.rem(3 * p + slot, 16)
         source = lax.div(left, 4) * 4 + lax.rem(lax.div(left, 2), 2)
-        for i in range(4):
-            for c in range(2):
-                from_z = lax.rem(zl + i, 4)
-                at = 4 * c + from_z
-                copy = pltpu.make_async_remote_copy(
-                    src_ref=fs.at[0, 0],
-                    dst_ref=fr.at[slot, at],
-                    send_sem=fs_sem.at[0, 0],
-                    recv_sem=fr_sem.at[slot, at],
-                    device_id={"frame": 4 * from_z + y, "patch": source + 2 * c},
-                    device_id_type=MESH,
-                )
-                if i > 0:
-                    copy.wait_recv()
-                else:
-
-                    @pl.when(source + 2 * c != p)
-                    def _():
-                        copy.wait_recv()
+        for c in range(2):
+            at = 4 * c + zl
+            copy = pltpu.make_async_remote_copy(
+                src_ref=fs.at[0, 0],
+                dst_ref=fr.at[slot, at],
+                send_sem=fs_sem.at[0],
+                recv_sem=fr_sem.at[2 * slot + c],
+                device_id={"patch": source + 2 * c},
+                device_id_type=MESH,
+            )
+
+            @pl.when(source + 2 * c != p)
+            def _():
+                copy.wait_recv()
+
+    for ref, sem in ((fs.at[pl.ds(0, 3)], fs_sem.at[6]), (fr.at[:, pl.ds(0, 6)], fr_sem.at[6])):
+        pltpu.make_async_copy(ref, ref, sem).wait()
 
     cols = []
     for slot in range(3):
@@ -670,6 +697,9 @@
             jnp.concatenate([total[:24, 36 * r : 36 * r + 36] for r in range(3)], axis=0)
         )
     gqs[...] = jnp.concatenate(cols, axis=-1)
+    writes[4].start()
+    for write in writes:
+        write.wait()
 
 
 def hand_over(*refs):
@@ -697,9 +727,11 @@
             jax.ShapeDtypeStruct((72, 108), F32),
             jax.ShapeDtypeStruct((36, 72), F32),
         ),
-        in_specs=[vmem] * 4 + [hbm] * 4,
-        out_specs=(vmem,) * 5,
+        in_specs=[hbm] * 8,
+        out_specs=(hbm,) * 5,
         scratch_shapes=[
+            buf(2, 64, D), buf(2, 64, D), wide(3, 2, D), wide(3, 2, D),
+            buf(2, 64, D), wide(72, 108), wide(36, 72), wide(72, 108), wide(36, 72), dma((9,)),
             buf(QKV, D), buf(ATT, D), buf(QKV, D), buf(ATT, D), dma((4,)),
             buf(2, 64, D), wide(128, QKV),
             buf(16, 16, 896), buf(16, 16, 896),
@@ -711,24 +743,24 @@
             buf(16, 16, 384), buf(16, 16, 384),
             buf(16, 16, 640), buf(16, 16, 640),
             buf(16, 16, 896), buf(16, 16, 896), buf(16, 64, 224), buf(1152, 1024),
-            dma((9, 2, 16)),
-            buf(1024, HD), buf(1024, HD), buf(1024, HD), wide(1024, 2),
+            dma((9, 2)),
+            buf(1024, HD), buf(1024, HD), buf(1024, HD), wide(1024, 2), wide(1024, 1), wide(1, 1024),
             buf(1024, HD), buf(128, 1024), wide(1024, HD), wide(1024, HD), wide(1024, HD),
             buf(2, 4, 2, 64, D), dma((2, 5)),
-            buf(8, 128, D), dma((2, 4)), buf(8, 128, 256), buf(8, 128, 256), dma((2, 8)),
-            buf(2, 128, 1280), buf(2, 128, 1280), buf(2, 128, 1280), dma((2, 2)),
-            buf(1280, 256),
+            buf(8, 128, D), dma((2, 4)), buf(8, 128, 256), buf(8, 128, 256), dma((2,)),
+            buf(2, 2, 128, 640), buf(2, 2, 128, 640), buf(2, 2, 128, 640), dma((2, 4)),
+            buf(640, 256),
             buf(4, 288, 256), buf(4, 288, 256),
             buf(4, 160, 640), buf(4, 160, 640),
             buf(4, 160, 256), buf(4, 160, 256),
             buf(4, 144, 640), buf(4, 144, 640),
             buf(4, 144, 256), buf(4, 144, 256),
             buf(4, 288, 224), buf(4, 288, 224),
-            dma((6, 2, 4)),
-            buf(8, 80, 128), buf(8, 80, 128),
-            buf(8, 80, 128), buf(8, 80, 128),
-            dma((2, 2, 8)),
-            buf(4, 6, 32, 128), buf(3, 8, 32, 128), dma((4, 6)), dma((3, 8)),
+            dma((6, 2)),
+            buf(8, 64, 128), buf(8, 64, 128),
+            buf(8, 48, 128), buf(8, 48, 128),
+            dma((2, 2)),
+            buf(4, 6, 32, 128), buf(3, 8, 32, 128), dma((7,)), dma((7,)),
         ],
         compiler_params=pltpu.CompilerParams(
             collective_id=0, has_side_effects=True, vmem_limit_bytes=60 * 1024 * 1024

time: 119 us -> 108 us (0.908); the launches traced: 119 us -> 106 us
  Pallas kernels: 118 us -> 106 us
    pallas_call x1, Pallas kernels: 116 us -> 104 us  [body(): pl.pallas_call(kernel, out_shape=(jax.ShapeDtypeStruct((2, 64, D), BF), j...]
where the time goes in v3:
time: 108 us; the launch traced here: 106 us
  Pallas kernels  106 us (98%)
    pallas_call x1, Pallas kernels, body(): pl.pallas_call(kernel, out_shape=(jax.ShapeDtypeStruct((2, 64, D), BF), j...  104 us

profile of v3, /device:TPU:32, one launch (start us, length us, event | category | flops | bytes accessed | tf_op | source)
XLA Modules:
  0.0 106.2 jit_solution(7571616194849344288)
XLA Ops:
  0.6 103.8 %shard_map.119 = (bf16[2,64,1152]{2,1,0:T(8,128)(2,1)}, f32[72,108]{1,0:T(8,128)}, f32[36,72]{1,0:T(8,128)}, f32[72,108]{1,0:T(8,128)}, f32[36,72]{1,0:T(8,128)}) custom-call(bf16[2,64,1152]{2,1,0:T(8,128)(2,1)} %bitcast.11, bf16[2,64,1152]{2,1,0:T(8,128)(2,1)} %bitcast.12, f32[3,2,1152]{2,1,0:T(2,128)} %bitcast.13, f32[3,2,1152]{2,1,0:T(2,128)} %bitcast.14, ...), custom_call_target="tpu_custom_call" | custom-call | tf_op jit(solution)/shard_map/pallas_call | solution.py:721
  104.5 1.8 %shard_map.120 = (bf16[2,64,1152]{2,1,0:T(8,128)(2,1)}, f32[72,108]{1,0:T(8,128)}, f32[36,72]{1,0:T(8,128)}, f32[72,108]{1,0:T(8,128)}, f32[36,72]{1,0:T(8,128)}) custom-call(bf16[2,64,1152]{2,1,0:T(8,128)(2,1)} %get-tuple-element.15.refs_0_, f32[72,108]{1,0:T(8,128)} %get-tuple-element.16.refs_1_, f32[36,72]{1,0:T(8,128)} %get-tuple-element.17.refs_2_, ...), custom_call_target="tpu_custom_call" | custom-call | tf_op jit(solution)/shard_map/pallas_call | solution.py:778

commit v4 on v3

--- a/solution.py
+++ b/solution.py
@@ -59,8 +59,8 @@
     return x.astype(BF).astype(F32)
 
 
-def zeros(*shape):
-    return jnp.zeros(shape, F32)
+def zeros(*shape, dtype=F32):
+    return jnp.zeros(shape, dtype)
 
 
 def fold(x, near):
@@ -77,7 +77,7 @@
 
 
 def widen(x, width):
-    return jnp.concatenate([x, zeros(x.shape[0], width - x.shape[1])], axis=-1)
+    return jnp.concatenate([x, zeros(x.shape[0], width - x.shape[1], dtype=x.dtype)], axis=-1)
 
 
 class Exchange:
@@ -116,8 +116,8 @@
     wqs, wos, wqt, wot, wsem,
     normed, proj,
     a_s, a_r, b1_s, b1_r, att_s, scaled, dmid, t1_s, t1_r, t2_s, t2_r,
-    c2_s, c2_r, c1_s, c1_r, dm_s, dm_r, d_s, d_r, dg, ngt, xsems,
-    q_b, k_b, v_b, rqk, rl, rrow, do_b, kt_b, dq_f, dk_f, dv_f,
+    c2_s, c2_r, c1_s, c1_r, dm_s, dm_r, dq_s, dq_r, d_s, d_r, dgq, dg, ngt, xsems,
+    q_b, k_b, v_b, rqk, rl, rrow, do_b, kt_b, dk_f, dv_f,
     ng, ngsem, xn, xnsem, dt_s, dt_r, dtsem,
     xl, xrv, xr, xsem, lt,
     syq, ryq, syo, ryo, sxo, rxo, sxs, rxs, sys, rys, gys, gyr, sem4,
@@ -214,6 +214,7 @@
     ex_c2 = Exchange(c2_s, c2_r, xsems.at[5, 0], xsems.at[5, 1], 16, f, on_frame)
     ex_c1 = Exchange(c1_s, c1_r, xsems.at[6, 0], xsems.at[6, 1], 16, p, on_patch)
     ex_dm = Exchange(dm_s, dm_r, xsems.at[7, 0], xsems.at[7, 1], 16, f, on_frame)
+    ex_dq = Exchange(dq_s, dq_r, xsems.at[2, 0], xsems.at[2, 1], 16, p, on_patch)
     ex_d = Exchange(d_s, d_r, xsems.at[8, 0], xsems.at[8, 1], 16, p, on_patch)
     ex_dt = Exchange(dt_s, dt_r, dtsem.at[0], dtsem.at[1], 8, 4 * core + x, on_column)
     ex_yq = Exchange(syq, ryq, sem4.at[0, 0], sem4.at[0, 1], 4, y, on_y)
@@ -246,10 +247,10 @@
         row = jnp.where(lane == 217, rq - rounded(rq), row)
         row = jnp.where(lane == 218, rk, row)
         row = jnp.where(lane == 219, rk - rounded(rk), row)
-        row = row.reshape(2, 4, 16, 224)
+        row = row.astype(BF).reshape(2, 4, 16, 224)
         for c in range(2):
             quarters = [row[c, j] for j in range(4)]
-            a_s[owner(c, h)] = jnp.concatenate(quarters, axis=-1).astype(BF)
+            a_s[owner(c, h)] = jnp.concatenate(quarters, axis=-1)
     pl.semaphore_wait(barrier, 75)
     ex_a.start()
 
@@ -271,19 +272,21 @@
         device_id={"patch": 4 * x + 2 * (1 - zh) + core},
         device_id_type=MESH,
     )
+    ex_t2.start()
     ex_a.wait()
     gather_z.start()
 
     for part in range(4):
-        rows = a_r[4 * part : 4 * part + 4].astype(F32)
+        rows = a_r[4 * part : 4 * part + 4]
         rows = [rows[:, :, 224 * j : 224 * j + 224] for j in range(4)]
         rows = jnp.stack(rows, axis=1).reshape(256, 224)
         at = pl.ds(256 * part, 256)
-        q_b[at, :] = rows[:, 0:HD].astype(BF)
-        k_b[at, :] = rows[:, HD : 2 * HD].astype(BF)
-        v_b[at, :] = rows[:, 2 * HD : 3 * HD].astype(BF)
-        rqk[at, 0:1] = rows[:, 216:217] + rows[:, 217:218]
-        rqk[at, 1:2] = rows[:, 218:219] + rows[:, 219:220]
+        q_b[at, :] = rows[:, 0:HD]
+        k_b[at, :] = rows[:, HD : 2 * HD]
+        v_b[at, :] = rows[:, 2 * HD : 3 * HD]
+        r = rows[:, 216:220].astype(F32)
+        rqk[at, 0:1] = r[:, 0:1] + r[:, 1:2]
+        rqk[at, 1:2] = r[:, 2:3] + r[:, 3:4]
 
     def attend(i, carry):
         part = lax.rem(x + 1 + i, 4)
@@ -291,9 +294,9 @@
         e = jnp.exp2(nt(q_b[at, :], k_b[...]) * (SCALE * LOG2E))
         r = 1.0 / jnp.sum(e, axis=-1, keepdims=True)
         rl[at, :] = r
-        pieces = (nn(e.astype(BF), v_b[...]) * r).reshape(4, 4, 16, HD)
-        row = [pieces[:, j].reshape(64, HD) for j in range(4)] + [zeros(64, 96)]
-        row = jnp.concatenate(row, axis=-1).astype(BF).reshape(4, 16, 384)
+        pieces = (nn(e.astype(BF), v_b[...]) * r).astype(BF).reshape(4, 4, 16, HD)
+        row = [pieces[:, j].reshape(64, HD) for j in range(4)] + [zeros(64, 96, dtype=BF)]
+        row = jnp.concatenate(row, axis=-1).reshape(4, 16, 384)
         b1_s[pl.ds(4 * part, 4)] = row
         for j in range(4):
             to = 4 * part + j
@@ -306,7 +309,6 @@
 
     lax.fori_loop(0, 4, attend, 0)
     b1_r[p] = b1_s[p]
-    ex_t2.start()
     for part in range(4):
         at = pl.ds(256 * part, 256)
         rrow[:, at] = jnp.transpose(widen(rl[at, :], 128))[0:1, :]
@@ -314,13 +316,13 @@
     ex_b1.wait()
     atts = []
     for c in range(2):
-        blocks = [b1_r[owner(c, h)].astype(F32) for h in range(HEADS)]
+        blocks = [b1_r[owner(c, h)] for h in range(HEADS)]
         rows = [
             jnp.concatenate([b[:, HD * j : HD * j + HD] for b in blocks], axis=-1)
             for j in range(4)
         ]
         atts.append(jnp.concatenate(rows, axis=0))
-    att_s[...] = jnp.concatenate(atts, axis=0).astype(BF)
+    att_s[...] = jnp.concatenate(atts, axis=0)
     added = nn(att_s[...], wos[...])
     for c in range(2):
         middle = lat[c].astype(F32) + mod_s[2, c : c + 1, :] * added[64 * c : 64 * c + 64]
@@ -364,16 +366,16 @@
         for yy in range(4):
             for zz in range(4):
                 at = 36 * (4 * zz + yy)
-                parts += [a[:, at : at + 36], zeros(128, 4)]
+                parts += [a[:, at : at + 36], zeros(128, 4, dtype=BF)]
         return parts
 
     def core_columns(full, cc):
         parts = [full[:, HD * (2 * b + cc) : HD * (2 * b + cc) + HD] for b in range(8)]
-        return jnp.concatenate(parts + [zeros(128, 64)], axis=-1).astype(BF)
-
-    xl[1, core] = jnp.concatenate(spread_rows(att_s[...].astype(F32)), axis=-1).astype(BF)
+        return jnp.concatenate(parts + [zeros(128, 64, dtype=BF)], axis=-1)
+
+    xl[1, core] = jnp.concatenate(spread_rows(att_s[...]), axis=-1)
     for cc in range(2):
-        xrv[0, cc] = core_columns(scaled[...].reshape(128, D).astype(F32), cc)
+        xrv[0, cc] = core_columns(scaled[...].reshape(128, D), cc)
     xr[0, core] = xrv[0, core]
 
     def pair_copies(which, slot):
@@ -454,8 +456,9 @@
         dq_parts.append(head_back(rounded(nn(ds, k.astype(BF))), q, rq))
         dk_parts.append(head_back(rounded(tn(ds, q.astype(BF))), k, rk))
         dv_parts.append(tn(soft.astype(BF), do))
-    dproj_t = jnp.concatenate(dq_parts + dk_parts + dv_parts, axis=-1)
-    dn = nn(dproj_t.astype(BF), wqt[...])
+    parts = [part.astype(BF) for part in dq_parts + dk_parts + dv_parts]
+    dproj_t = jnp.concatenate(parts, axis=-1)
+    dn = nn(dproj_t, wqt[...])
     back = normalise_back(dn, stretch_t, xh_t, r_t)
     dm_s[...] = fold(back.reshape(16, 8, D), 640).astype(BF)
     ex_dm.start()
@@ -463,14 +466,14 @@
     for cc in range(2):
         for xx in range(4):
             at = 108 * (4 * xx + cc)
-            row = [dproj_t[:, at : at + 108], zeros(128, 20)]
-            row += [dproj_t[:, at + 216 : at + 324], zeros(128, 20)]
-            dt_s[4 * cc + xx] = jnp.concatenate(row, axis=-1).astype(BF)
+            row = [dproj_t[:, at : at + 108], zeros(128, 20, dtype=BF)]
+            row += [dproj_t[:, at + 216 : at + 324], zeros(128, 20, dtype=BF)]
+            dt_s[4 * cc + xx] = jnp.concatenate(row, axis=-1)
     ex_dt.start()
 
     ex_c2.wait()
     att_t = unfold(c2_r[...].astype(F32), ATT).reshape(128, ATT)
-    xl[0, core] = jnp.concatenate(spread_rows(att_t), axis=-1).astype(BF)
+    xl[0, core] = jnp.concatenate(spread_rows(att_t.astype(BF)), axis=-1)
     for copy in pair_copies(0, core):
         copy.start()
     for i in range(1, 4):
@@ -486,7 +489,10 @@
     gather_core(True).wait()
     for i in range(8):
         block = ng[i // 4, i % 4].reshape(128, D).astype(F32)
-        ngt[:, 128 * i : 128 * i + 128] = jnp.transpose(block).astype(BF)
+        block = jnp.transpose(block).reshape(4, 4, HD, 128)
+        for yy in range(4):
+            rows = block[:, yy].reshape(288, 128)
+            ngt[288 * yy : 288 * yy + 288, 128 * i : 128 * i + 128] = rows.astype(BF)
 
     ex_dm.wait()
     back = unfold(dm_r[...].astype(F32), D).reshape(2, 64, D)
@@ -496,16 +502,16 @@
         dmid[c] = total.astype(BF)
         parts.append((total * mod_s[2, c : c + 1, :]).astype(BF))
     scaled_s = jnp.concatenate(parts, axis=0)
-    tokens = nt(scaled_s, wos[...]).reshape(2, 64, ATT)
+    tokens = nt(scaled_s, wos[...]).astype(BF).reshape(2, 64, ATT)
     for c in range(2):
         for h in range(HEADS):
             part = tokens[c][:, HD * h : HD * h + HD].reshape(4, 16, HD)
-            row = jnp.concatenate([part[j] for j in range(4)] + [zeros(16, 96)], axis=-1)
-            c1_s[owner(c, h)] = row.astype(BF)
+            row = [part[j] for j in range(4)] + [zeros(16, 96, dtype=BF)]
+            c1_s[owner(c, h)] = jnp.concatenate(row, axis=-1)
     ex_c1.start()
 
     for cc in range(2):
-        xrv[1, cc] = core_columns(scaled_s.astype(F32), cc)
+        xrv[1, cc] = core_columns(scaled_s, cc)
     xr[1, core] = xrv[1, core]
     for copy in pair_copies(1, core):
         copy.start()
@@ -531,14 +537,15 @@
         sxo[i] = widen(total[:, 144 * i : 144 * i + 144], 256).astype(BF)
     ex_xo.start()
     ex_c1.wait()
-    got_do = c1_r[...].astype(F32)
+    got_do = c1_r[...]
     parts = [got_do[:, :, HD * j : HD * j + HD] for j in range(4)]
-    do_b[...] = (jnp.stack(parts, axis=1).reshape(1024, HD) * rl[...]).astype(BF)
+    do_b[...] = (jnp.stack(parts, axis=1).reshape(1024, HD).astype(F32) * rl[...]).astype(BF)
     dk_f[...] = jnp.zeros_like(dk_f)
     dv_f[...] = jnp.zeros_like(dv_f)
 
     def attend_back(i, carry):
-        at = pl.ds(pl.multiple_of(i * 256, 256), 256)
+        part = lax.rem(x + 1 + i, 4)
+        at = pl.ds(pl.multiple_of(part * 256, 256), 256)
         qb, dob = q_b[at, :], do_b[at, :]
         e = jnp.exp2(nt(k_b[...], qb) * (SCALE * LOG2E))
         dp = nt(v_b[...], dob)
@@ -546,31 +553,52 @@
         ds = (e * (dp - shift)).astype(BF)
         dv_f[...] += nn(e.astype(BF), dob)
         dk_f[...] += nn(ds, qb)
-        dq_f[at, :] = jnp.transpose(nn(kt_b[...], ds))[:, :HD]
+        dq = rounded(jnp.transpose(nn(kt_b[...], ds))[:, :HD] * SCALE)
+        dq = head_back(dq, qb.astype(F32), rqk[at, 0:1]).astype(BF)
+        blocks = pl.ds(4 * part, 4)
+        dgq[blocks] = dq.reshape(4, 64, HD)
+        dq = dq.reshape(4, 4, 16, HD)
+        row = [dq[:, j].reshape(64, HD) for j in range(4)] + [zeros(64, 96, dtype=BF)]
+        dq_s[blocks] = jnp.concatenate(row, axis=-1).reshape(4, 16, 384)
+        for j in range(4):
+            to = 4 * part + j
+
+            @pl.when(to != p)
+            def _():
+                ex_dq.copy(to, p).start()
+
         return carry
 
     lax.fori_loop(0, 4, attend_back, 0)
+    dq_r[p] = dq_s[p]
     for part in range(4):
         at = pl.ds(256 * part, 256)
-        dq = head_back(rounded(dq_f[at, :] * SCALE), q_b[at, :].astype(F32), rqk[at, 0:1])
         dk = head_back(rounded(dk_f[at, :] * SCALE), k_b[at, :].astype(F32), rqk[at, 1:2])
-        row = jnp.concatenate([dq, dk, dv_f[at, :], zeros(256, 8)], axis=-1)
-        dg[4 * part : 4 * part + 4] = row.astype(BF).reshape(4, 64, 224)
-        row = row.reshape(4, 4, 16, 224)
-        row = jnp.concatenate([row[:, j].reshape(64, 224) for j in range(4)], axis=-1)
-        d_s[4 * part : 4 * part + 4] = row.astype(BF).reshape(4, 16, 896)
+        row = jnp.concatenate([dk.astype(BF), dv_f[at, :].astype(BF)], axis=-1)
+        dg[4 * part : 4 * part + 4] = row.reshape(4, 64, 2 * HD)
+        row = row.reshape(4, 4, 16, 2 * HD)
+        row = [row[:, j].reshape(64, 2 * HD) for j in range(4)] + [zeros(64, 64, dtype=BF)]
+        d_s[4 * part : 4 * part + 4] = jnp.concatenate(row, axis=-1).reshape(4, 16, 640)
     ex_d.start()
+
+    order = [4 * xx + 2 * s + cc for cc in range(2) for xx in range(4) for s in range(2)]
+    right = [jnp.concatenate([ref[i] for i in order], axis=0) for ref in (dgq, dg)]
+    right = jnp.concatenate(right + [zeros(1024, 8, dtype=BF)], axis=-1)
+    for i in range(1, 5):
+        yy = lax.rem(y + i, 4)
+        rows = pl.ds(pl.multiple_of(288 * yy, 288), 288)
+        gys[yy] = nn(ngt[rows, :], right).astype(BF)
+        if i < 4:
+            ex_gy.copy(yy, y).start()
+    gyr[y] = gys[y]
     ex_xs.wait()
     total = sum(rxs[i].astype(F32) for i in range(4))
     for i in range(4):
-        sys[i] = widen(total[:, 160 * i : 160 * i + 160], 256).astype(BF)
+        part = total[:, 160 * i : 160 * i + 160]
+        rest = [part[48 * j : 48 * j + 48, 128:] for j in range(3)] + [zeros(48, 32)]
+        rest = jnp.concatenate(rest, axis=-1)
+        sys[i] = jnp.concatenate([part[:, :128], rest], axis=0).astype(BF)
     ex_ys.start()
-
-    blocks = [dg[4 * xx + 2 * s + cc] for cc in range(2) for xx in range(4) for s in range(2)]
-    g = nn(ngt[...], jnp.concatenate(blocks, axis=0)).reshape(4, 4, HD, 224)
-    for yy in range(4):
-        gys[yy] = g[:, yy].reshape(288, 224).astype(BF)
-    ex_gy.start()
     ex_yq.wait()
     total = sum(ryq[i].astype(F32) for i in range(4))
     for i in range(8):
@@ -581,19 +609,6 @@
         szq[i] = jnp.concatenate([part[:64], rest, zeros(64, 2)], axis=-1).astype(BF)
     ex_zq.start()
 
-
-    ex_xo.wait()
-    ex_ys.wait()
-    total = sum(rxo[i].astype(F32) for i in range(4))
-    other = sum(rys[i].astype(F32) for i in range(4))
-    other = jnp.transpose(jnp.concatenate([other, zeros(112, 256)], axis=0))
-    for i in range(8):
-        zz, s = i % 4, i // 4
-        rows, cols = slice(40 * zz, 40 * zz + 36), slice(HD * s, HD * s + HD)
-        part = jnp.concatenate([total[rows, cols], other[rows, cols]], axis=0)
-        rest = jnp.concatenate([part[48:, :36], part[48:, 36:]], axis=0)
-        szo[i] = jnp.concatenate([part[:48], rest, zeros(48, 20)], axis=-1).astype(BF)
-    ex_zo.start()
 
     ex_gy.wait()
     total = sum(gyr[i].astype(F32) for i in range(4)).reshape(4, 3, 24, 224)
@@ -631,15 +646,33 @@
                 def _():
                     fr[slot, z] = fs[zl, b]
 
+    ex_xo.wait()
+    ex_ys.wait()
+    total = sum(rxo[i].astype(F32) for i in range(4))
+    other = sum(rys[i].astype(F32) for i in range(4))
+    rest = jnp.concatenate([other[144:, 32 * j : 32 * j + 32] for j in range(3)], axis=0)
+    other = widen(jnp.concatenate([other[:144], rest], axis=-1), 256)
+    other = jnp.transpose(jnp.concatenate([other, zeros(112, 256)], axis=0))
+    for i in range(8):
+        zz, s = i % 4, i // 4
+        rows, cols = slice(40 * zz, 40 * zz + 36), slice(HD * s, HD * s + HD)
+        part = jnp.concatenate([total[rows, cols], other[rows, cols]], axis=0)
+        rest = jnp.concatenate([part[48:, :36], part[48:, 36:]], axis=0)
+        szo[i] = jnp.concatenate([part[:48], rest, zeros(48, 20)], axis=-1).astype(BF)
+    ex_zo.start()
+
+    ex_dq.wait()
     ex_d.wait()
     parts = []
     for c in range(2):
-        blocks = [d_r[owner(c, h)].astype(F32) for h in range(HEADS)]
+        firsts = [dq_r[owner(c, h)] for h in range(HEADS)]
+        blocks = [d_r[owner(c, h)] for h in range(HEADS)]
         for i in range(4):
-            at = [224 * i + HD * j for j in range(3)]
-            row = [b[:, a : a + HD] for a in at for b in blocks]
+            row = [b[:, HD * i : HD * i + HD] for b in firsts]
+            at = [2 * HD * i + HD * j for j in range(2)]
+            row += [b[:, a : a + HD] for a in at for b in blocks]
             parts.append(jnp.concatenate(row, axis=-1))
-    dn = nn(jnp.concatenate(parts, axis=0).astype(BF), wqs[...])
+    dn = nn(jnp.concatenate(parts, axis=0), wqs[...])
     for c in range(2):
         xh, r = normalise(lat[c].astype(F32))
         back = normalise_back(dn[64 * c : 64 * c + 64], mod_s[1, c : c + 1, :], xh, r)
@@ -703,12 +736,19 @@
 
 
 def hand_over(*refs):
-    for src, dst in zip(refs[:5], refs[5:]):
-        dst[...] = src[...]
+    given, out, held, sem = refs[:5], refs[5:10], refs[10:15], refs[15]
+    into = [pltpu.make_async_copy(given[i], held[i], sem.at[0, i]) for i in range(5)]
+    back = [pltpu.make_async_copy(held[i], out[i], sem.at[1, i]) for i in range(5)]
+    for copy in into:
+        copy.start()
+    for i in range(5):
+        into[i].wait()
+        back[i].start()
+    for copy in back:
+        copy.wait()
 
 
 def body(lat, mod_s, mod_t, wqs, wos, wqt, wot, cot):
-    vmem = pl.BlockSpec(memory_space=pltpu.VMEM)
     hbm = pl.BlockSpec(memory_space=pl.ANY)
     dma = pltpu.SemaphoreType.DMA
 
@@ -742,10 +782,11 @@
             buf(16, 16, 384), buf(16, 16, 384),
             buf(16, 16, 384), buf(16, 16, 384),
             buf(16, 16, 640), buf(16, 16, 640),
-            buf(16, 16, 896), buf(16, 16, 896), buf(16, 64, 224), buf(1152, 1024),
+            buf(16, 16, 384), buf(16, 16, 384), buf(16, 16, 640), buf(16, 16, 640),
+            buf(16, 64, HD), buf(16, 64, 2 * HD), buf(1152, 1024),
             dma((9, 2)),
             buf(1024, HD), buf(1024, HD), buf(1024, HD), wide(1024, 2), wide(1024, 1), wide(1, 1024),
-            buf(1024, HD), buf(128, 1024), wide(1024, HD), wide(1024, HD), wide(1024, HD),
+            buf(1024, HD), buf(128, 1024), wide(1024, HD), wide(1024, HD),
             buf(2, 4, 2, 64, D), dma((2, 5)),
             buf(8, 128, D), dma((2, 4)), buf(8, 128, 256), buf(8, 128, 256), dma((2,)),
             buf(2, 2, 128, 640), buf(2, 2, 128, 640), buf(2, 2, 128, 640), dma((2, 4)),
@@ -754,7 +795,7 @@
             buf(4, 160, 640), buf(4, 160, 640),
             buf(4, 160, 256), buf(4, 160, 256),
             buf(4, 144, 640), buf(4, 144, 640),
-            buf(4, 144, 256), buf(4, 144, 256),
+            buf(4, 192, 128), buf(4, 192, 128),
             buf(4, 288, 224), buf(4, 288, 224),
             dma((6, 2)),
             buf(8, 64, 128), buf(8, 64, 128),
@@ -778,8 +819,9 @@
     outs = pl.pallas_call(
         hand_over,
         out_shape=tuple(jax.ShapeDtypeStruct(o.shape, o.dtype) for o in outs),
-        in_specs=[vmem] * 5,
-        out_specs=(vmem,) * 5,
+        in_specs=[hbm] * 5,
+        out_specs=(hbm,) * 5,
+        scratch_shapes=[pltpu.VMEM(o.shape, o.dtype) for o in outs] + [dma((2, 5))],
     )(*outs)
     return (outs[0].reshape(2, 1, 64, D),) + tuple(outs[1:])
 

time: 108 us -> 106 us (0.981); the launches traced: 106 us -> 106 us
  no operation moved by 1% of the time
where the time goes in v4:
time: 106 us
  Pallas kernels  105 us (99%)
    pallas_call x1, Pallas kernels, body(): pl.pallas_call(kernel, out_shape=(jax.ShapeDtypeStruct((2, 64, D), BF), j...  103 us

profile of v4, /device:TPU:32, one launch (start us, length us, event | category | flops | bytes accessed | tf_op | source)
XLA Modules:
  0.0 105.8 jit_solution(211045643060824562)
XLA Ops:
  0.6 103.2 %shard_map.119 = (bf16[2,64,1152]{2,1,0:T(8,128)(2,1)}, f32[72,108]{1,0:T(8,128)}, f32[36,72]{1,0:T(8,128)}, f32[72,108]{1,0:T(8,128)}, f32[36,72]{1,0:T(8,128)}) custom-call(bf16[2,64,1152]{2,1,0:T(8,128)(2,1)} %bitcast.11, bf16[2,64,1152]{2,1,0:T(8,128)(2,1)} %bitcast.12, f32[3,2,1152]{2,1,0:T(2,128)} %bitcast.13, f32[3,2,1152]{2,1,0:T(2,128)} %bitcast.14, ...), custom_call_target="tpu_custom_call" | custom-call | tf_op jit(solution)/shard_map/pallas_call | solution.py:761
  103.8 1.8 %shard_map.120 = (bf16[2,64,1152]{2,1,0:T(8,128)(2,1)}, f32[72,108]{1,0:T(8,128)}, f32[36,72]{1,0:T(8,128)}, f32[72,108]{1,0:T(8,128)}, f32[36,72]{1,0:T(8,128)}) custom-call(bf16[2,64,1152]{2,1,0:T(8,128)(2,1)} %get-tuple-element.15.refs_0_, f32[72,108]{1,0:T(8,128)} %get-tuple-element.16.refs_1_, f32[36,72]{1,0:T(8,128)} %get-tuple-element.17.refs_2_, ...), custom_call_target="tpu_custom_call" | custom-call | tf_op jit(solution)/shard_map/pallas_call | solution.py:819

commit v5 on v4

--- a/solution.py
+++ b/solution.py
@@ -440,7 +440,8 @@
         rk = inverse_norm(k)
         q = q * rq
         k = k * rk
-        e = jnp.where(same, jnp.exp(nt(q.astype(BF), k.astype(BF)) * SCALE), 0.0)
+        e = nt(q.astype(BF), k.astype(BF)) * (SCALE * LOG2E)
+        e = jnp.where(same, jnp.exp2(e), 0.0)
         soft = e * (1.0 / jnp.sum(e, axis=-1, keepdims=True))
         att_parts.append(nn(soft.astype(BF), v))
         heads.append((q, k, v, rq, rk, soft))
@@ -531,11 +532,6 @@
     for yy in range(4):
         syq[yy] = g[:, yy].reshape(288, 256).astype(BF)
     ex_yq.start()
-    ex_yo.wait()
-    total = sum(ryo[i].astype(F32) for i in range(4))
-    for i in range(4):
-        sxo[i] = widen(total[:, 144 * i : 144 * i + 144], 256).astype(BF)
-    ex_xo.start()
     ex_c1.wait()
     got_do = c1_r[...]
     parts = [got_do[:, :, HD * j : HD * j + HD] for j in range(4)]
@@ -544,8 +540,8 @@
     dv_f[...] = jnp.zeros_like(dv_f)
 
     def attend_back(i, carry):
-        part = lax.rem(x + 1 + i, 4)
-        at = pl.ds(pl.multiple_of(part * 256, 256), 256)
+        part = lax.rem(lax.div(x, 2) + 1 + i, 2)
+        at = pl.ds(pl.multiple_of(part * 512, 512), 512)
         qb, dob = q_b[at, :], do_b[at, :]
         e = jnp.exp2(nt(k_b[...], qb) * (SCALE * LOG2E))
         dp = nt(v_b[...], dob)
@@ -555,13 +551,13 @@
         dk_f[...] += nn(ds, qb)
         dq = rounded(jnp.transpose(nn(kt_b[...], ds))[:, :HD] * SCALE)
         dq = head_back(dq, qb.astype(F32), rqk[at, 0:1]).astype(BF)
-        blocks = pl.ds(4 * part, 4)
-        dgq[blocks] = dq.reshape(4, 64, HD)
-        dq = dq.reshape(4, 4, 16, HD)
-        row = [dq[:, j].reshape(64, HD) for j in range(4)] + [zeros(64, 96, dtype=BF)]
-        dq_s[blocks] = jnp.concatenate(row, axis=-1).reshape(4, 16, 384)
-        for j in range(4):
-            to = 4 * part + j
+        blocks = pl.ds(8 * part, 8)
+        dgq[blocks] = dq.reshape(8, 64, HD)
+        dq = dq.reshape(8, 4, 16, HD)
+        row = [dq[:, j].reshape(128, HD) for j in range(4)] + [zeros(128, 96, dtype=BF)]
+        dq_s[blocks] = jnp.concatenate(row, axis=-1).reshape(8, 16, 384)
+        for j in range(8):
+            to = 8 * part + j
 
             @pl.when(to != p)
             def _():
@@ -569,7 +565,7 @@
 
         return carry
 
-    lax.fori_loop(0, 4, attend_back, 0)
+    lax.fori_loop(0, 2, attend_back, 0)
     dq_r[p] = dq_s[p]
     for part in range(4):
         at = pl.ds(256 * part, 256)
@@ -591,6 +587,11 @@
         if i < 4:
             ex_gy.copy(yy, y).start()
     gyr[y] = gys[y]
+    ex_yo.wait()
+    total = sum(ryo[i].astype(F32) for i in range(4))
+    for i in range(4):
+        sxo[i] = widen(total[:, 144 * i : 144 * i + 144], 256).astype(BF)
+    ex_xo.start()
     ex_xs.wait()
     total = sum(rxs[i].astype(F32) for i in range(4))
     for i in range(4):

time: 106 us -> 106 us (level)
  no operation moved by 1% of the time
where the time goes in v5:
time: 106 us
  Pallas kernels  105 us (99%)
    pallas_call x1, Pallas kernels, body(): pl.pallas_call(kernel, out_shape=(jax.ShapeDtypeStruct((2, 64, D), BF), j...  103 us

profile of v5, /device:TPU:32, one launch (start us, length us, event | category | flops | bytes accessed | tf_op | source)
XLA Modules:
  0.0 105.5 jit_solution(13117132402144199803)
XLA Ops:
  0.6 102.9 %shard_map.119 = (bf16[2,64,1152]{2,1,0:T(8,128)(2,1)}, f32[72,108]{1,0:T(8,128)}, f32[36,72]{1,0:T(8,128)}, f32[72,108]{1,0:T(8,128)}, f32[36,72]{1,0:T(8,128)}) custom-call(bf16[2,64,1152]{2,1,0:T(8,128)(2,1)} %bitcast.11, bf16[2,64,1152]{2,1,0:T(8,128)(2,1)} %bitcast.12, f32[3,2,1152]{2,1,0:T(2,128)} %bitcast.13, f32[3,2,1152]{2,1,0:T(2,128)} %bitcast.14, ...), custom_call_target="tpu_custom_call" | custom-call | tf_op jit(solution)/shard_map/pallas_call | solution.py:762
  103.6 1.8 %shard_map.120 = (bf16[2,64,1152]{2,1,0:T(8,128)(2,1)}, f32[72,108]{1,0:T(8,128)}, f32[36,72]{1,0:T(8,128)}, f32[72,108]{1,0:T(8,128)}, f32[36,72]{1,0:T(8,128)}) custom-call(bf16[2,64,1152]{2,1,0:T(8,128)(2,1)} %get-tuple-element.15.refs_0_, f32[72,108]{1,0:T(8,128)} %get-tuple-element.16.refs_1_, f32[36,72]{1,0:T(8,128)} %get-tuple-element.17.refs_2_, ...), custom_call_target="tpu_custom_call" | custom-call | tf_op jit(solution)/shard_map/pallas_call | solution.py:820

commit v6 on v5

--- a/solution.py
+++ b/solution.py
@@ -587,11 +587,6 @@
         if i < 4:
             ex_gy.copy(yy, y).start()
     gyr[y] = gys[y]
-    ex_yo.wait()
-    total = sum(ryo[i].astype(F32) for i in range(4))
-    for i in range(4):
-        sxo[i] = widen(total[:, 144 * i : 144 * i + 144], 256).astype(BF)
-    ex_xo.start()
     ex_xs.wait()
     total = sum(rxs[i].astype(F32) for i in range(4))
     for i in range(4):
@@ -600,6 +595,11 @@
         rest = jnp.concatenate(rest, axis=-1)
         sys[i] = jnp.concatenate([part[:, :128], rest], axis=0).astype(BF)
     ex_ys.start()
+    ex_yo.wait()
+    total = sum(ryo[i].astype(F32) for i in range(4))
+    for i in range(4):
+        sxo[i] = widen(total[:, 144 * i : 144 * i + 144], 256).astype(BF)
+    ex_xo.start()
     ex_yq.wait()
     total = sum(ryq[i].astype(F32) for i in range(4))
     for i in range(8):
@@ -611,6 +611,8 @@
     ex_zq.start()
 
 
+    ex_xo.wait()
+    first = sum(rxo[i].astype(F32) for i in range(4))
     ex_gy.wait()
     total = sum(gyr[i].astype(F32) for i in range(4)).reshape(4, 3, 24, 224)
     for b in range(6):
@@ -647,9 +649,7 @@
                 def _():
                     fr[slot, z] = fs[zl, b]
 
-    ex_xo.wait()
     ex_ys.wait()
-    total = sum(rxo[i].astype(F32) for i in range(4))
     other = sum(rys[i].astype(F32) for i in range(4))
     rest = jnp.concatenate([other[144:, 32 * j : 32 * j + 32] for j in range(3)], axis=0)
     other = widen(jnp.concatenate([other[:144], rest], axis=-1), 256)
@@ -657,7 +657,7 @@
     for i in range(8):
         zz, s = i % 4, i // 4
         rows, cols = slice(40 * zz, 40 * zz + 36), slice(HD * s, HD * s + HD)
-        part = jnp.concatenate([total[rows, cols], other[rows, cols]], axis=0)
+        part = jnp.concatenate([first[rows, cols], other[rows, cols]], axis=0)
         rest = jnp.concatenate([part[48:, :36], part[48:, 36:]], axis=0)
         szo[i] = jnp.concatenate([part[:48], rest, zeros(48, 20)], axis=-1).astype(BF)
     ex_zo.start()

time: 106 us -> 106 us (level)
  no operation moved by 1% of the time
where the time goes in v6:
time: 106 us
  Pallas kernels  105 us (99%)
    pallas_call x1, Pallas kernels, body(): pl.pallas_call(kernel, out_shape=(jax.ShapeDtypeStruct((2, 64, D), BF), j...  103 us

profile of v6, /device:TPU:32, one launch (start us, length us, event | category | flops | bytes accessed | tf_op | source)
XLA Modules:
  0.0 105.9 jit_solution(12975789912250751927)
XLA Ops:
  0.6 103.3 %shard_map.119 = (bf16[2,64,1152]{2,1,0:T(8,128)(2,1)}, f32[72,108]{1,0:T(8,128)}, f32[36,72]{1,0:T(8,128)}, f32[72,108]{1,0:T(8,128)}, f32[36,72]{1,0:T(8,128)}) custom-call(bf16[2,64,1152]{2,1,0:T(8,128)(2,1)} %bitcast.11, bf16[2,64,1152]{2,1,0:T(8,128)(2,1)} %bitcast.12, f32[3,2,1152]{2,1,0:T(2,128)} %bitcast.13, f32[3,2,1152]{2,1,0:T(2,128)} %bitcast.14, ...), custom_call_target="tpu_custom_call" | custom-call | tf_op jit(solution)/shard_map/pallas_call | solution.py:762
  103.9 1.8 %shard_map.120 = (bf16[2,64,1152]{2,1,0:T(8,128)(2,1)}, f32[72,108]{1,0:T(8,128)}, f32[36,72]{1,0:T(8,128)}, f32[72,108]{1,0:T(8,128)}, f32[36,72]{1,0:T(8,128)}) custom-call(bf16[2,64,1152]{2,1,0:T(8,128)(2,1)} %get-tuple-element.15.refs_0_, f32[72,108]{1,0:T(8,128)} %get-tuple-element.16.refs_1_, f32[36,72]{1,0:T(8,128)} %get-tuple-element.17.refs_2_, ...), custom_call_target="tpu_custom_call" | custom-call | tf_op jit(solution)/shard_map/pallas_call | solution.py:820
